TPU v7x, 128 devices: a whole 4x4x4 slice. The times are simulated.
128 devices in a mesh: dp: 64 (over z, x_lo, y, core), fsdp: 2 (over x_hi).
Axes of the slice: x: 4 (x_hi: 2, x_lo: 2; x = x_hi * 2 + x_lo), y: 4, z: 4, core: 2. Of those that a mesh axis runs over, the one named last changes fastest.
Arguments:
- tokens: bfloat16 [128, 256, 384], P(('dp', 'fsdp')), may hold values from -24 to 24
- condition: bfloat16 [128, 384], P(('dp', 'fsdp')), may hold values from -24 to 24
- modulation_weight: bfloat16 [1, 384, 2304], P(None, ('dp', 'fsdp')), may hold values from -0.3125 to 0.3125
- modulation_bias: bfloat16 [1, 2304], P(None, ('dp', 'fsdp')), may hold values from -3 to 3
- attend_weight: bfloat16 [1, 384, 1152], P(None, ('dp', 'fsdp')), may hold values from -0.3125 to 0.3125
- attend_bias: bfloat16 [1, 768], P(None, ('dp', 'fsdp')), may hold values from -3 to 3
- output_weight: bfloat16 [1, 384, 384], P(None, ('dp', 'fsdp')), may hold values from -1.25 to 1.25
- output_bias: bfloat16 [1, 384], P(None, ('dp', 'fsdp')), may hold values from -2 to 2
- up_weight: bfloat16 [1, 384, 1536], P(None, ('dp', 'fsdp')), may hold values from -0.3125 to 0.3125
- up_bias: bfloat16 [1, 1536], P(None, ('dp', 'fsdp')), may hold values from -3 to 3
- down_weight: bfloat16 [1, 1536, 384], P(None, ('dp', 'fsdp')), may hold values from -0.15625 to 0.15625
- down_bias: bfloat16 [1, 384], P(None, ('dp', 'fsdp')), may hold values from -2 to 2
- cotangent: bfloat16 [128, 256, 384], P(('dp', 'fsdp')), may hold values from -6 to 6
Outputs:
- result: bfloat16 [128, 256, 384], P(('dp', 'fsdp'))
- token_grad: float32 [128, 256, 384], P(('dp', 'fsdp'))
- condition_grad: float32 [128, 384], P(('dp', 'fsdp'))
- modulation_weight_grad: float32 [1, 384, 2304], P(None, ('dp', 'fsdp'))
- modulation_bias_grad: float32 [1, 2304], P(None, ('dp', 'fsdp'))
- attend_weight_grad: float32 [1, 384, 1152], P(None, ('dp', 'fsdp'))
- attend_bias_grad: float32 [1, 768], P(None, ('dp', 'fsdp'))
- output_weight_grad: float32 [1, 384, 384], P(None, ('dp', 'fsdp'))
- output_bias_grad: float32 [1, 384], P(None, ('dp', 'fsdp'))
- up_weight_grad: float32 [1, 384, 1536], P(None, ('dp', 'fsdp'))
- up_bias_grad: float32 [1, 1536], P(None, ('dp', 'fsdp'))
- down_weight_grad: float32 [1, 1536, 384], P(None, ('dp', 'fsdp'))
- down_bias_grad: float32 [1, 384], P(None, ('dp', 'fsdp'))
All inputs are finite; a program needn't handle non-finite values.
Results may differ from a plain program's by a relative error of at most 0.02.
The roundings to bfloat16 on the way count: a program that leaves them out, or rounds other values in their place, can miss the bound.
Values may be sent and summed in bfloat16 or wider, within the bound.
A program may use at most 128 MiB of HBM per device.

v0:
```python
import jax
import jax.numpy as jnp
from jax import lax
from jax.sharding import PartitionSpec as P

HEADS = 6
HEAD = 64


EPS = 1e-06


def normalize(stream):
    center = jnp.mean(stream, axis=-1, keepdims=True)
    shifted = stream - center
    spread = jnp.mean(shifted * shifted, axis=-1, keepdims=True)
    return shifted * lax.rsqrt(spread + EPS)


def modulate(stream, shift, scale):
    return normalize(stream) * (1.0 + scale) + shift


def gelu_tanh(values):
    return jax.nn.gelu(values, approximate=True)


def product(left, right):
    return jnp.dot(left, right, preferred_element_type=jnp.float32)


def product_left(left, right):
    return lax.dot_general(
        left, right, (((0,), (0,)), ((), ())), preferred_element_type=jnp.float32
    )


def product_right(left, right):
    return lax.dot_general(
        left, right, (((1,), (1,)), ((), ())), preferred_element_type=jnp.float32
    )


def fetch_forward(shards, layer_index):
    return (
        lax.all_gather(shards[0][layer_index], ("dp", "fsdp"), axis=0, tiled=True),
        lax.all_gather(shards[1][layer_index], ("dp", "fsdp"), axis=0, tiled=True),
        lax.all_gather(shards[2][layer_index], ("dp", "fsdp"), axis=0, tiled=True),
        lax.all_gather(shards[3][layer_index], ("dp", "fsdp"), axis=0, tiled=True),
        lax.all_gather(shards[4][layer_index], ("dp", "fsdp"), axis=0, tiled=True),
        lax.all_gather(shards[5][layer_index], ("dp", "fsdp"), axis=0, tiled=True),
        lax.all_gather(shards[6][layer_index], ("dp", "fsdp"), axis=0, tiled=True),
        lax.all_gather(shards[7][layer_index], ("dp", "fsdp"), axis=0, tiled=True),
        lax.all_gather(shards[8][layer_index], ("dp", "fsdp"), axis=0, tiled=True),
        lax.all_gather(shards[9][layer_index], ("dp", "fsdp"), axis=0, tiled=True),
    )


def fetch_backward(shards, layer_index):
    return (
        lax.all_gather(shards[0][layer_index], ("dp", "fsdp"), axis=0, tiled=True),
        lax.all_gather(shards[1][layer_index], ("dp", "fsdp"), axis=0, tiled=True),
        lax.all_gather(shards[2][layer_index], ("dp", "fsdp"), axis=0, tiled=True),
        lax.all_gather(shards[3][layer_index], ("dp", "fsdp"), axis=0, tiled=True),
        lax.all_gather(shards[4][layer_index], ("dp", "fsdp"), axis=0, tiled=True),
        lax.all_gather(shards[5][layer_index], ("dp", "fsdp"), axis=0, tiled=True),
        lax.all_gather(shards[6][layer_index], ("dp", "fsdp"), axis=0, tiled=True),
        lax.all_gather(shards[7][layer_index], ("dp", "fsdp"), axis=0, tiled=True),
        lax.all_gather(shards[8][layer_index], ("dp", "fsdp"), axis=0, tiled=True),
        lax.all_gather(shards[9][layer_index], ("dp", "fsdp"), axis=0, tiled=True),
    )


def split_triple(triple, token_count, model_width):
    queries = triple[:, :model_width].reshape(token_count, HEADS, HEAD)
    keys_all = triple[:, model_width : 2 * model_width].reshape(token_count, HEADS, HEAD)
    values_all = triple[:, 2 * model_width :].reshape(token_count, HEADS, HEAD)
    return (queries, keys_all, values_all)


def layer_forward(stream, cact_row, weights):
    (
        w_modulation,
        b_modulation,
        w_attend,
        b_attend,
        w_output,
        b_output,
        w_up,
        b_up,
        w_down,
        b_down,
    ) = weights
    token_count = stream.shape[0]
    model_width = stream.shape[1]
    factor = HEAD ** (-0.5)
    modulation = product(cact_row[None, :], w_modulation)[0] + b_modulation.astype(jnp.float32)
    shift_one, scale_one, gate_one, shift_two, scale_two, gate_two = jnp.split(modulation, 6)
    hidden_one = modulate(stream, shift_one, scale_one).astype(jnp.bfloat16)
    attend_float = b_attend.astype(jnp.float32)
    zero_keys = jnp.zeros((model_width,), jnp.float32)
    bias_full = jnp.concatenate([attend_float[:model_width], zero_keys, attend_float[model_width:]])
    triple = (product(hidden_one, w_attend) + bias_full).astype(jnp.bfloat16)
    queries, keys_all, values_all = split_triple(triple, token_count, model_width)
    scores = (
        jnp.einsum("qhd,khd->hqk", queries, keys_all, preferred_element_type=jnp.float32) * factor
    )
    highest = jnp.max(scores, axis=-1, keepdims=True)
    exponent = jnp.exp(scores - highest)
    row_total = jnp.sum(exponent, axis=-1, keepdims=True)
    probabilities = exponent / row_total
    logsum = highest + jnp.log(row_total)
    mixed_heads = (
        jnp.einsum(
            "hqk,khd->qhd",
            probabilities.astype(jnp.bfloat16),
            values_all,
            preferred_element_type=jnp.float32,
        )
        .reshape(token_count, model_width)
        .astype(jnp.bfloat16)
    )
    branch = product(mixed_heads, w_output) + b_output.astype(jnp.float32)
    middle = stream + gate_one * branch
    hidden_two = modulate(middle, shift_two, scale_two).astype(jnp.bfloat16)
    upper_in = product(hidden_two, w_up) + b_up.astype(jnp.float32)
    activated = gelu_tanh(upper_in).astype(jnp.bfloat16)
    feed_out = product(activated, w_down) + b_down.astype(jnp.float32)
    outcome = middle + gate_two * feed_out
    stored = (
        stream,
        modulation,
        hidden_one,
        triple,
        logsum,
        mixed_heads,
        branch,
        middle,
        hidden_two,
        upper_in,
        activated,
        feed_out,
    )
    return (outcome, stored)


def layer_backward(gradient, cact_row, weights, stored):
    (
        w_modulation,
        b_modulation,
        w_attend,
        b_attend,
        w_output,
        b_output,
        w_up,
        b_up,
        w_down,
        b_down,
    ) = weights
    (
        stream,
        modulation,
        hidden_one,
        triple,
        logsum,
        mixed_heads,
        branch,
        middle,
        hidden_two,
        upper_in,
        activated,
        feed_out,
    ) = stored
    token_count = stream.shape[0]
    model_width = stream.shape[1]
    factor = HEAD ** (-0.5)
    shift_one, scale_one, gate_one, shift_two, scale_two, gate_two = jnp.split(modulation, 6)
    delta_gate_two = jnp.sum(gradient * feed_out, axis=0)
    delta_feed = (gate_two * gradient).astype(jnp.bfloat16)
    delta_w_down = product_left(activated, delta_feed)
    delta_b_down = jnp.sum(delta_feed.astype(jnp.float32), axis=0)
    delta_activated = product_right(delta_feed, w_down)
    _, gelu_pull = jax.vjp(gelu_tanh, upper_in)
    delta_upper = gelu_pull(delta_activated)[0].astype(jnp.bfloat16)
    delta_w_up = product_left(hidden_two, delta_upper)
    delta_b_up = jnp.sum(delta_upper.astype(jnp.float32), axis=0)
    delta_hidden_two = product_right(delta_upper, w_up)
    _, second_pull = jax.vjp(modulate, middle, shift_two, scale_two)
    delta_middle, delta_shift_two, delta_scale_two = second_pull(delta_hidden_two)
    gradient_mid = gradient + delta_middle
    delta_gate_one = jnp.sum(gradient_mid * branch, axis=0)
    delta_branch = (gate_one * gradient_mid).astype(jnp.bfloat16)
    delta_w_output = product_left(mixed_heads, delta_branch)
    delta_b_output = jnp.sum(delta_branch.astype(jnp.float32), axis=0)
    delta_mixed = (
        product_right(delta_branch, w_output).astype(jnp.bfloat16).reshape(token_count, HEADS, HEAD)
    )
    queries, keys_all, values_all = split_triple(triple, token_count, model_width)
    scores = (
        jnp.einsum("qhd,khd->hqk", queries, keys_all, preferred_element_type=jnp.float32) * factor
    )
    probabilities = jnp.exp(scores - logsum)
    delta_probs = jnp.einsum(
        "qhd,khd->hqk", delta_mixed, values_all, preferred_element_type=jnp.float32
    )
    delta_values = jnp.einsum(
        "hqk,qhd->khd",
        probabilities.astype(jnp.bfloat16),
        delta_mixed,
        preferred_element_type=jnp.float32,
    )
    row_inner = jnp.sum(probabilities * delta_probs, axis=-1, keepdims=True)
    delta_scores = (probabilities * (delta_probs - row_inner)).astype(jnp.bfloat16)
    delta_queries = (
        jnp.einsum("hqk,khd->qhd", delta_scores, keys_all, preferred_element_type=jnp.float32)
        * factor
    )
    delta_keys = (
        jnp.einsum("hqk,qhd->khd", delta_scores, queries, preferred_element_type=jnp.float32)
        * factor
    )
    delta_triple = jnp.concatenate(
        [
            delta_queries.reshape(token_count, model_width),
            delta_keys.reshape(token_count, model_width),
            delta_values.reshape(token_count, model_width),
        ],
        axis=1,
    ).astype(jnp.bfloat16)
    delta_w_attend = product_left(hidden_one, delta_triple)
    column_sums = jnp.sum(delta_triple.astype(jnp.float32), axis=0)
    delta_b_attend = jnp.concatenate([column_sums[:model_width], column_sums[2 * model_width :]])
    delta_hidden_one = product_right(delta_triple, w_attend)
    _, first_pull = jax.vjp(modulate, stream, shift_one, scale_one)
    delta_stream, delta_shift_one, delta_scale_one = first_pull(delta_hidden_one)
    gradient_in = gradient_mid + delta_stream
    delta_modulation = jnp.concatenate(
        [
            delta_shift_one,
            delta_scale_one,
            delta_gate_one,
            delta_shift_two,
            delta_scale_two,
            delta_gate_two,
        ]
    )
    delta_w_modulation = cact_row.astype(jnp.float32)[:, None] * delta_modulation[None, :]
    leading_part = delta_modulation.astype(jnp.bfloat16)
    trailing_part = (delta_modulation - leading_part.astype(jnp.float32)).astype(jnp.bfloat16)
    delta_cact = (
        product_right(leading_part[None, :], w_modulation)[0]
        + product_right(trailing_part[None, :], w_modulation)[0]
    )
    layer_grads = (
        delta_w_modulation,
        delta_modulation,
        delta_w_attend,
        delta_b_attend,
        delta_w_output,
        delta_b_output,
        delta_w_up,
        delta_b_up,
        delta_w_down,
        delta_b_down,
    )
    return (gradient_in, delta_cact, layer_grads)


def local(
    tokens,
    condition,
    modulation_weight,
    modulation_bias,
    attend_weight,
    attend_bias,
    output_weight,
    output_bias,
    up_weight,
    up_bias,
    down_weight,
    down_bias,
    cotangent,
):
    shards = (
        modulation_weight,
        modulation_bias,
        attend_weight,
        attend_bias,
        output_weight,
        output_bias,
        up_weight,
        up_bias,
        down_weight,
        down_bias,
    )
    layers = modulation_weight.shape[0]
    devices = lax.axis_size(("dp", "fsdp"))
    first_member = 0
    accumulated = [None] * 10
    for member in range(first_member, 10):
        shard_piece = shards[member]
        accumulated[member] = jnp.zeros(
            (layers, shard_piece.shape[1] * devices) + shard_piece.shape[2:], jnp.float32
        )
    condition_float = condition.astype(jnp.float32)
    silu_values, silu_pull = jax.vjp(jax.nn.silu, condition_float)
    cact = silu_values.astype(jnp.bfloat16)
    modulation_grads = []
    stream = tokens[0].astype(jnp.float32)
    layer_index = 0
    weights = fetch_forward(shards, layer_index)
    stream, stored = layer_forward(stream, cact[0], weights)
    retained = [(weights, stored)]
    outputs = [stream.astype(jnp.bfloat16)]
    gradient = cotangent[0].astype(jnp.float32)
    cact_total = jnp.zeros((cact.shape[1],), jnp.float32)
    latent_modulation = [None] * layers
    for layer_index in reversed(range(layers)):
        weights = fetch_backward(shards, layer_index)
        gradient, delta_cact, layer_grads = layer_backward(
            gradient, cact[0], weights, retained[layer_index][1]
        )
        cact_total = delta_cact
        latent_modulation[layer_index] = layer_grads[1]
        for member in range(first_member, 10):
            accumulated[member] = accumulated[member].at[layer_index].add(layer_grads[member])
    token_grads = [gradient]
    cact_grads = [cact_total]
    modulation_grads.append(jnp.stack(latent_modulation))
    condition_grad = silu_pull(jnp.stack(cact_grads))[0]
    reduced_all = tuple(
        (
            lax.psum_scatter(accumulated[0], ("dp", "fsdp"), scatter_dimension=1, tiled=True),
            lax.psum_scatter(accumulated[1], ("dp", "fsdp"), scatter_dimension=1, tiled=True),
            lax.psum_scatter(accumulated[2], ("dp", "fsdp"), scatter_dimension=1, tiled=True),
            lax.psum_scatter(accumulated[3], ("dp", "fsdp"), scatter_dimension=1, tiled=True),
            lax.psum_scatter(accumulated[4], ("dp", "fsdp"), scatter_dimension=1, tiled=True),
            lax.psum_scatter(accumulated[5], ("dp", "fsdp"), scatter_dimension=1, tiled=True),
            lax.psum_scatter(accumulated[6], ("dp", "fsdp"), scatter_dimension=1, tiled=True),
            lax.psum_scatter(accumulated[7], ("dp", "fsdp"), scatter_dimension=1, tiled=True),
            lax.psum_scatter(accumulated[8], ("dp", "fsdp"), scatter_dimension=1, tiled=True),
            lax.psum_scatter(accumulated[9], ("dp", "fsdp"), scatter_dimension=1, tiled=True),
        )
    )
    return (jnp.stack(outputs), jnp.stack(token_grads), condition_grad) + tuple(reduced_all)


def solution(mesh):
    return jax.shard_map(
        local,
        mesh=mesh,
        in_specs=(
            P(("dp", "fsdp"), None, None),
            P(("dp", "fsdp"), None),
            P(None, ("dp", "fsdp"), None),
            P(None, ("dp", "fsdp")),
            P(None, ("dp", "fsdp"), None),
            P(None, ("dp", "fsdp")),
            P(None, ("dp", "fsdp"), None),
            P(None, ("dp", "fsdp")),
            P(None, ("dp", "fsdp"), None),
            P(None, ("dp", "fsdp")),
            P(None, ("dp", "fsdp"), None),
            P(None, ("dp", "fsdp")),
            P(("dp", "fsdp"), None, None),
        ),
        out_specs=(
            P(("dp", "fsdp"), None, None),
            P(("dp", "fsdp"), None, None),
            P(("dp", "fsdp"), None),
            P(None, ("dp", "fsdp"), None),
            P(None, ("dp", "fsdp")),
            P(None, ("dp", "fsdp"), None),
            P(None, ("dp", "fsdp")),
            P(None, ("dp", "fsdp"), None),
            P(None, ("dp", "fsdp")),
            P(None, ("dp", "fsdp"), None),
            P(None, ("dp", "fsdp")),
            P(None, ("dp", "fsdp"), None),
            P(None, ("dp", "fsdp")),
        ),
        check_vma=False,
    )
```

profile of v0, /device:TPU:1, one launch (start us, length us, event | category | flops | bytes accessed | tf_op | source)
XLA Modules:
  0.0 1146.5 jit_solution(12592650609321488245)
XLA Ops:
  7.2 1.4 copy.71
  8.7 1.3 copy.78
  10.1 1.3 copy.79
  11.5 1.0 convert_reduce_fusion.2
  12.6 1.1 fusion.55
  13.7 0.6 copy-done.35
  14.3 0.7 convert_reduce_fusion.5
  15.6 0.7 copy.77
  16.3 0.8 dynamic-update-slice.22
  17.1 0.8 dynamic-update-slice.24
  18.0 0.8 dynamic-update-slice.21
  18.8 0.8 dynamic-update-slice.23
  19.6 0.8 dynamic-update-slice.20
  20.5 69.1 %all-reduce.17 = (bf16[768]{0:T(1024)(128)(2,1)S(1)}, bf16[2304]{0:T(1024)(128)(2,1)S(1)}, bf16[384]{0:T(512)(128)(2,1)S(1)}, bf16[384]{0:T(512)(128)(2,1)S(1)}, bf16[1536]{0:T(1024)(128)(2,1)S(1)}) all-reduce(bf16[768]{0:T(1024)(128)(2,1)S(1)} %dynamic-update-slice.21, ...), channel_id=5, replica_groups=mesh['dp'=64,'fsdp'=2] {'dp','fsdp'}, use_global_device_ids=true, to_apply=%add.1 | all-reduce | flops 5376 | bytes 21504
  89.6 0.6 convert_element_type.157
  90.2 0.6 convert_element_type.159
  90.8 0.7 copy.72
  91.5 312.3 %all-gather.4 = bf16[1,384,384]{2,0,1:T(2,128)(2,1)S(1)} all-gather(bf16[1,3,384]{2,0,1:T(2,128)(2,1)S(1)} %copy.77), channel_id=6, replica_groups=mesh['dp'=64,'fsdp'=2] {'dp','fsdp'}, dimensions={1}, use_global_device_ids=true | all-gather | bytes 297216 | tf_op jit(solution)/shard_map/all_gather | solution.py:50
  403.8 323.0 %all-gather.2 = bf16[1,384,1152]{2,0,1:T(2,128)(2,1)S(1)} all-gather(bf16[1,3,1152]{2,0,1:T(2,128)(2,1)S(1)} %copy.72), channel_id=4, replica_groups=mesh['dp'=64,'fsdp'=2] {'dp','fsdp'}, dimensions={1}, use_global_device_ids=true | all-gather | bytes 891648 | tf_op jit(solution)/shard_map/all_gather | solution.py:48
  726.8 3.0 fusion.26
  729.8 0.6 fusion.84
  731.0 0.6 fusion
  733.4 1.1 fusion.81
  735.1 0.6 copy-done.37
  735.6 0.6 fusion.73
  736.3 3.5 convolution_add_fusion.1
  739.7 187.4 %all-gather.18.cloned.1.call-done = bf16[1,1536,384]{2,0,1:T(2,128)(2,1)} async-done(((bf16[1,12,384]{2,0,1:T(2,128)(2,1)}), bf16[1,1536,384]{2,0,1:T(2,128)(2,1)}) %all-gather.18.cloned.1.call-update) | async-done | bytes 1179664 | tf_op jit(solution)/shard_map/all_gather | solution.py:54
  927.1 4.4 convert_reduce_fusion
  931.6 1.2 multiply_reduce_fusion.1
  933.1 0.7 convert_reduce_fusion.4
  933.9 1.0 convolution_convert_fusion
  935.1 1.1 copy.80
  938.1 0.8 copy-done.9
  939.0 0.8 convolution_bitcast_fusion
  939.8 0.7 copy-done.3
  940.5 0.6 fusion.56
  941.2 0.6 convolution_bitcast_fusion.2
  942.3 0.6 convolution_bitcast_fusion.1
  943.0 1.4 copy.85
  944.7 8.4 copy.87
  953.1 3.0 copy.84
  956.2 3.8 copy.86
  960.1 2.4 convert_reduce_fusion.3
  962.6 3.7 broadcast_multiply_fusion
  966.3 0.6 scatter-add.30
  966.9 1.6 scatter-add.40
  968.5 0.6 scatter-add.36
  969.1 1.2 scatter-add.44
  970.4 1.4 convert_reduce_fusion.1
  971.7 0.6 scatter-add.34
  972.4 0.6 fusion.32
  973.0 0.6 fusion.29
  973.6 66.1 %all-reduce.15 = (f32[1,2304]{1,0:T(1,128)S(1)}, f32[1,768]{1,0:T(1,128)S(1)}, f32[1,384]{1,0:T(1,128)S(1)}, f32[1,1536]{1,0:T(1,128)S(1)}, f32[1,384]{1,0:T(1,128)S(1)}) all-reduce(f32[1,2304]{1,0:T(1,128)S(1)} %copy-done.17, f32[1,768]{1,0:T(1,128)} %scatter-add.34, ...), channel_id=13, replica_groups=mesh['dp'=64,'fsdp'=2] {'dp','fsdp'}, use_global_device_ids=true, to_apply=%region_18.19.clone | all-reduce | flops 5376 | bytes 43008
  1039.7 0.6 constant_dynamic-slice_fusion.8
  1040.3 0.6 constant_dynamic-slice_fusion.6
  1040.9 0.6 constant_dynamic-slice_fusion.2
  1041.5 0.6 constant_dynamic-slice_fusion
  1042.1 1.2 fusion.69
  1043.3 90.1 %all-reduce.20.cloned.1.call-done = (f32[1,384,2304]{2,0,1:T(1,128)}, f32[1,384,1152]{2,0,1:T(1,128)}, f32[1,384,384]{2,0,1:T(1,128)}, f32[1,384,1536]{2,0,1:T(1,128)}, f32[1,1536,384]{2,0,1:T(1,128)}) async-done(((f32[1,384,2304]{2,0,1:T(1,128)}, f32[1,384,1152]{2,0,1:T(1,128)}, f32[1,384,384]{2,0,1:T(1,128)}, f32[1,384,1536]{2,0,1:T(1,128)}, f32[1,1536,384]{2,0,1:T(1,128)}), (f32[1,384,2304]{2,0,1:T(1,128)}, ...) | async-done | bytes 10616848
  1133.4 1.4 constant_dynamic-slice_fusion.9
  1134.7 1.3 constant_dynamic-slice_fusion.5
  1136.0 1.3 constant_dynamic-slice_fusion.7
  1137.3 1.3 constant_dynamic-slice_fusion.3
  1138.7 1.3 constant_dynamic-slice_fusion.1
  (157 shorter events, 7.3 us)
Async XLA Ops:
  7.2 719.7 %copy-start.30 = (bf16[1,384]{1,0:T(2,128)(2,1)S(1)}, bf16[1,384]{1,0:T(2,128)(2,1)}, u32[]{:S(2)}) copy-start(bf16[1,384]{1,0:T(2,128)(2,1)} %param.34) | copy-start | bytes 2308
  7.2 719.6 %all-gather.14.cloned.1.call-start = ((), (), s32[]{:S(2)}) async-start(), calls=%async_computation | async-start | bytes 3566592 | tf_op jit(solution)/shard_map/all_gather | solution.py:46
  8.6 727.6 %all-gather.16.cloned.1.call-start = ((), (), s32[]{:S(2)}) async-start(), calls=%async_computation.1 | async-start | bytes 2377728 | tf_op jit(solution)/shard_map/all_gather | solution.py:52
  10.0 917.1 %all-gather.18.cloned.1.call-start = ((), (), s32[]{:S(2)}) async-start(), calls=%async_computation.2 | async-start | bytes 2377728 | tf_op jit(solution)/shard_map/all_gather | solution.py:54
  11.4 1122.0 %all-reduce.20.cloned.1.call-start = ((), (), s32[]{:S(2)}) async-start(), calls=%async_computation.3 | async-start | bytes 21233664
  12.6 717.9 %copy-start.26 = (f32[256]{0:T(256)}, f32[256]{0:T(256)S(1)}, u32[]{:S(2)}) copy-start(f32[256]{0:T(256)S(1)} %broadcast_multiply_fusion.2) | copy-start | bytes 3076
  13.7 0.6 copy-start.35
  14.3 716.1 %copy-start.33 = (f32[256]{0:T(256)}, f32[256]{0:T(256)S(1)}, u32[]{:S(2)}) copy-start(f32[256]{0:T(256)S(1)} %fusion.72) | copy-start | bytes 3076
  15.0 714.8 %copy-start.32 = (f32[1,384]{1,0:T(1,128)}, f32[1,384]{1,0:T(1,128)S(1)}, u32[]{:S(2)}) copy-start(f32[1,384]{1,0:T(1,128)S(1)} %get-tuple-element.188) | copy-start | bytes 4612
  403.8 327.2 %copy-start.1 = (bf16[1,256,384]{2,1,0:T(8,128)(2,1)S(1)}, bf16[1,256,384]{2,1,0:T(8,128)(2,1)}, u32[]{:S(2)}) copy-start(bf16[1,256,384]{2,1,0:T(8,128)(2,1)} %param.33) | copy-start | bytes 589828
  726.8 4.8 copy-start.2
  730.4 0.6 copy-start.42
  730.4 1.2 copy-start.23
  730.4 2.7 copy-start.21
  732.8 0.7 copy-start.41
  734.5 0.5 copy-start.19
  735.1 0.6 copy-start.37
  927.1 4.4 copy-start.12
  927.1 4.4 copy-start.18
  927.1 4.4 copy-start.20
  927.1 4.4 copy-start.28
  931.5 1.3 copy-start.10
  931.6 1.2 copy-start.38
  931.6 1.5 copy-start.14
  931.6 1.5 copy-start.22
  933.1 1.8 copy-start.7
  933.1 1.8 copy-start.44
  936.6 4.6 copy-start.6
  937.5 1.5 copy-start.9
  937.5 1.5 copy-start.15
  937.5 1.5 copy-start.46
  937.9 3.3 copy-start.4
  939.0 2.2 copy-start.5
  939.0 1.5 copy-start.3
  939.0 1.5 copy-start.24
  939.0 1.5 copy-start.27
  940.5 0.7 copy-start.34
  940.5 0.7 copy-start.43
  941.2 1.1 copy-start.11
  941.2 1.1 copy-start.25
  941.2 1.1 copy-start.29
  942.3 2.1 copy-start.36
  956.2 3.9 copy-start.16
  956.2 3.9 copy-start.8
  956.2 3.9 copy-start.13
  956.2 3.9 copy-start.45
  956.2 3.9 copy-start.47
  956.2 3.9 copy-start.50
  960.1 2.4 copy-start.49
  960.1 2.4 copy-start.48
  960.1 2.4 copy-start.40
  966.3 2.3 copy-start.39
  966.3 6.1 copy-start
  972.4 1.2 copy-start.17
  972.4 69.7 %copy-start.31 = (bf16[1,384]{1,0:T(2,128)(2,1)S(1)}, bf16[1,384]{1,0:T(2,128)(2,1)}, u32[]{:S(2)}) copy-start(bf16[1,384]{1,0:T(2,128)(2,1)} %param.34) | copy-start | bytes 2308
Sparse Core Ops, SparseCore 0:
  10.3 309.4 all-gather.13
  322.0 301.8 all-gather.15
  626.2 300.8 all-gather.17
  966.4 166.9 all-reduce.19
where the time goes:
time: 1150 us
  blocking collectives  771 us (67%)
  waiting for transfers between devices  278 us (24%)
  local copies, waits for them, and re-layouts  46.2 us (4%)
  matrix products  23.4 us (2%)
  between operations  14.4 us (1%)
  other arithmetic  14.3 us (1%)
    all_gather x1, blocking collectives, fetch_forward(): lax.all_gather(shards[2][layer_index], ('dp', 'fsdp'), axis=0, tiled=True)  323 us
    all_gather x1, blocking collectives, fetch_forward(): lax.all_gather(shards[4][layer_index], ('dp', 'fsdp'), axis=0, tiled=True)  312 us
    all_gather x1, waiting for transfers between devices, fetch_forward(): lax.all_gather(shards[8][layer_index], ('dp', 'fsdp'), axis=0, tiled=True)  187 us
    unnamed x2, blocking collectives  135 us
    unnamed x5, waiting for transfers between devices  90.1 us
    unnamed x131, local copies, waits for them, and re-layouts  23.2 us
  transfers between devices with their start and end apart: 4, of which 2 were waited for; matrix products, arithmetic and copies ran while one was open for 3% of the time, Pallas kernels for 0%

commit v1 on v0

v1 whole, which is shorter than its diff:
```python
import functools

import jax
import jax.numpy as jnp
from jax import lax
from jax.experimental import pallas as pl
from jax.experimental.pallas import tpu as pltpu
from jax.sharding import PartitionSpec as P

MESH = pl.DeviceIdType.MESH
F32 = jnp.float32
BF16 = jnp.bfloat16
EPS = 1e-06
HEAD = 64
D = 384
FF = 1536
S = 256
FACTOR = HEAD ** (-0.5)
VMEM_LIMIT = 60 * 1024 * 1024

PARTS = 3
WIDE = 512
ORDERS = ((0, 1, 2), (1, 2, 0), (2, 0, 1))
BIASES = {"mod": (18, 0), "attend": (6, 18), "output": (3, 24), "up": (12, 27), "down": (3, 39)}


def dot(a, b, ca=1, cb=0):
    return lax.dot_general(a, b, (((ca,), (cb,)), ((), ())), preferred_element_type=F32)


def place():
    dp, fsdp = lax.axis_index("dp"), lax.axis_index("fsdp")
    core = lax.rem(dp, 2)
    y = lax.rem(lax.div(dp, 2), 4)
    x = lax.rem(lax.div(dp, 8), 2) + 2 * fsdp
    return (x, y, lax.div(dp, 16)), core


def device(at, core):
    x, y, z = at
    return (z * 16 + lax.rem(x, 2) * 8 + y * 2 + core, lax.div(x, 2))


def moved(at, axis, by):
    return tuple(lax.rem(c + by, 4) if i == axis else c for i, c in enumerate(at))


def slot_of(part, x, y, z, core):
    at = (x, y, z)
    a, b, c = ORDERS[part]
    return ((core * 4 + at[c]) * 4 + at[b]) * 4 + at[a]


def greet(at, core):
    barrier = pltpu.get_barrier_semaphore()
    for axis in range(3):
        for by in range(1, 4):
            pl.semaphore_signal(
                barrier, inc=1, device_id=device(moved(at, axis, by), core), device_id_type=MESH
            )
    pl.semaphore_signal(barrier, inc=1, device_id=device(at, 1 - core), device_id_type=MESH)
    pl.semaphore_wait(barrier, 10)


def remote(src, dst, send, recv, to):
    copy = pltpu.make_async_remote_copy(
        src_ref=src, dst_ref=dst, send_sem=send, recv_sem=recv, device_id=to, device_id_type=MESH
    )
    copy.start()
    return copy


def spread_rows(transposed):
    shape = (256, 256)
    n = lax.broadcasted_iota(jnp.int32, shape, 0 if transposed else 1)
    o = lax.broadcasted_iota(jnp.int32, shape, 1 if transposed else 0)
    member, row = n >> 4, n & 15
    section = (row * 11) >> 5
    target = jnp.where(row == 15, 240 + member, section * 48 + member * 3 + (row - 3 * section))
    return jnp.where(target == o, 1.0, 0.0).astype(BF16)


def spread_down(transposed):
    shape = (256, 192) if transposed else (192, 256)
    n = lax.broadcasted_iota(jnp.int32, shape, 0 if transposed else 1)
    o = lax.broadcasted_iota(jnp.int32, shape, 1 if transposed else 0)
    member, row = n >> 4, n & 15
    target = jnp.where(row < 12, member * 12 + row, -1)
    return jnp.where(target == o, 1.0, 0.0).astype(BF16)


def members(part, group):
    z, x_lo = group // 2, group % 2
    return [
        slot_of(part, 2 * x_hi + x_lo, y, z, core)
        for y in range(4)
        for core in range(2)
        for x_hi in range(2)
    ]


def gather_kernel(
    mod, b_mod, att, b_att, out, b_out, up, b_up, down, b_down,
    w_mod, w_att, w_out, w_up, w_down, bias,
    held, send1, recv1, send2, recv2, send3, recv3, send4, recv4, send_c, recv_c,
):
    at, core = place()

    def load(ref, lo, hi):
        return ref[0, :, lo:hi].astype(F32)

    row = jnp.concatenate(
        [ref[...].astype(F32) for ref in (b_mod, b_att, b_out, b_up, b_down)]
        + [jnp.zeros((1, 1152 - 42), F32)],
        axis=1,
    )
    main = jnp.concatenate(
        [
            load(mod, 0, 1152),
            load(mod, 1152, 2304),
            load(att, 0, 1152),
            load(up, 0, 1152),
            jnp.concatenate([load(up, 1152, 1536), load(out, 0, 384), jnp.zeros((3, 384), F32)], axis=1),
            row,
        ],
        axis=0,
    ).astype(BF16)
    rest = jnp.concatenate([load(down, 0, 384), jnp.zeros((4, 384), F32)], axis=0).astype(BF16)
    own = [slot_of(p, *at, core) for p in range(PARTS)]
    held[0, own[0]] = main[:, 0:512]
    held[1, own[1]] = main[:, 512:1024]
    held[2, own[2], :, 0:128] = main[:, 1024:1152]
    held[2, own[2], :, 128:512] = rest

    greet(at, core)
    copies = []

    def first(p):
        block = held.at[p, pl.ds(own[p], 1)]
        return [
            remote(block, block, send1.at[p, d - 1], recv1.at[p, d - 1], device(moved(at, ORDERS[p][0], d), core))
            for d in (1, 3, 2)
        ]

    def second(p):
        _, b, c = ORDERS[p]
        block = held.at[p, pl.ds(((core * 4 + at[c]) * 4 + at[b]) * 4, 4)]
        return [
            remote(block, block, send2.at[p, d - 1], recv2.at[p, d - 1], device(moved(at, b, d), core))
            for d in (1, 3, 2)
        ]

    def plane(p, by, lo=0, count=16):
        c = ORDERS[p][2]
        return held.at[p, pl.ds((core * 4 + lax.rem(at[c] + by, 4)) * 16 + lo, count)]

    def across(p, k, block):
        return remote(block, block, send_c.at[p, k], recv_c.at[p, k], device(at, 1 - core))

    stage1 = [first(p) for p in range(PARTS)]
    stage2 = []
    for p in range(PARTS):
        for copy in stage1[p]:
            copy.wait_recv()
        stage2.append(second(p))
    stage3 = []
    for p in range(PARTS):
        for copy in stage2[p]:
            copy.wait_recv()
        c = ORDERS[p][2]
        block = plane(p, 0)
        stage3.append(
            [
                remote(block, block, send3.at[p, k], recv3.at[p, k], device(moved(at, c, by), core))
                for k, by in enumerate((1, 3))
            ]
        )
        copies.append(across(p, 0, block))
    stage4 = []
    for p in range(PARTS):
        c = ORDERS[p][2]
        for k, by in enumerate((3, 1)):
            stage3[p][k].wait_recv()
            half = plane(p, by, 8 * k, 8)
            stage4.append(
                remote(half, half, send4.at[p, k], recv4.at[p, k], device(moved(at, c, 4 - by), core))
            )
            copies.append(across(p, 1 + k, plane(p, by)))
    for p in range(PARTS):
        for k in range(2):
            stage4[2 * p + k].wait_recv()
            copies.append(across(p, 3 + k, plane(p, 2, 8 * k, 8)))
    for copy in copies:
        copy.wait_recv()
    for copy in sum(stage1 + stage2 + stage3, []) + stage4 + copies:
        copy.wait_send()

    rows, rows_down = spread_rows(False), spread_down(False)
    for group in range(8):
        at48, at192, at16 = 48 * group, 192 * group, 16 * group
        for p in range(PARTS):
            blocks = jnp.concatenate([held[p, s] for s in members(p, group)], axis=0)
            wide = WIDE if p < 2 else 128
            laid = dot(rows, blocks[:, :wide]).astype(BF16)
            lo = WIDE * p
            here = slice(at48, at48 + 48)
            w_mod[here, lo : lo + wide] = laid[0:48]
            w_mod[here, 1152 + lo : 1152 + lo + wide] = laid[48:96]
            w_att[here, lo : lo + wide] = laid[96:144]
            w_up[here, lo : lo + wide] = laid[144:192]
            if p == 0:
                w_up[here, 1152:1536] = laid[192:240, 0:384]
                w_out[here, 0:128] = laid[192:240, 384:512]
                bias[at16 : at16 + 16, :] = laid[240:256, 0:128]
            if p == 1:
                w_out[here, 128:384] = laid[192:240, 0:256]
            if p == 2:
                w_down[at192 : at192 + 192, :] = dot(rows_down, blocks[:, 128:512]).astype(BF16)


def bias_map(name, count):
    size, lane = BIASES[name]
    n = lax.broadcasted_iota(jnp.int32, (128, count), 1)
    owner = (n * -(-65536 // size)) >> 16
    k = lax.broadcasted_iota(jnp.int32, (128, count), 0)
    return owner == k, (n - owner * size + lane) == k


def bias_row(bias, name, count):
    mine, lane = bias_map(name, count)
    picked = dot(bias, jnp.where(lane, 1.0, 0.0).astype(BF16))
    return jnp.sum(jnp.where(mine, picked, 0.0), axis=0, keepdims=True)


def bias_block(row, name):
    mine, lane = bias_map(name, row.shape[1])
    placed = jnp.where(mine, row, 0.0).astype(BF16)
    return dot(placed, jnp.where(lane, 1.0, 0.0).astype(BF16), 1, 1)


def normalize(v):
    shifted = v - jnp.mean(v, axis=-1, keepdims=True)
    inverse = lax.rsqrt(jnp.mean(shifted * shifted, axis=-1, keepdims=True) + EPS)
    return shifted * inverse, inverse


def denormalize(e, n, inverse):
    return inverse * (
        e - jnp.mean(e, axis=-1, keepdims=True) - n * jnp.mean(e * n, axis=-1, keepdims=True)
    )


def total(v):
    return jnp.sum(v, axis=0, keepdims=True)


def block_kernel(
    tokens, condition, cotangent, w_mod, w_att, w_out, w_up, w_down, bias,
    result, token_grad, condition_grad, packed,
    d_mod, d_att, d_out, d_up, d_down, probs_ref,
):
    x = tokens[0].astype(F32)
    g = cotangent[0].astype(F32)
    cond = condition[...].astype(F32)
    sigmoid = 1.0 / (1.0 + jnp.exp(-cond))
    cact = (cond * sigmoid).astype(BF16).astype(F32)
    cact_column = jnp.broadcast_to(cact, (128, D)).T
    raw_bias = bias[...]
    modulation = jnp.concatenate(
        [total(w_mod[:, 128 * t : 128 * t + 128].astype(F32) * cact_column) for t in range(18)],
        axis=1,
    ) + bias_row(raw_bias, "mod", 6 * D)
    shift1, scale1, gate1, shift2, scale2, gate2 = [
        modulation[:, D * i : D * i + D] for i in range(6)
    ]
    n1, inverse1 = normalize(x)
    hidden1 = (n1 * (1.0 + scale1) + shift1).astype(BF16)
    b_att = bias_row(raw_bias, "attend", 2 * D)
    b_full = jnp.concatenate([b_att[:, :D], jnp.zeros((1, D), F32), b_att[:, D:]], axis=1)
    triple = (dot(hidden1, w_att[...]) + b_full).astype(BF16)

    def pair(i, which):
        lo = D * which + 128 * i
        return triple[:, lo : lo + 128]

    lane = lax.broadcasted_iota(jnp.int32, (S, 128), 1)
    halves = [lane < 64, lane >= 64]
    nothing = jnp.zeros((S, 128), BF16)
    mixed_pairs = []
    keys_t = []
    for i in range(3):
        q, k, v = pair(i, 0), pair(i, 1), pair(i, 2)
        v_t = v.T
        keys_t.append(k.T)
        mixed_t = []
        for h in range(2):
            scores = dot(k, jnp.where(halves[h], q, nothing), 1, 1) * FACTOR
            e = jnp.exp(scores - jnp.max(scores, axis=0, keepdims=True))
            probs = e * (1.0 / total(e))
            probs_ref[2 * i + h] = probs
            mixed_t.append(dot(v_t[64 * h : 64 * h + 64], probs.astype(BF16)))
        mixed_pairs.append(jnp.concatenate(mixed_t, axis=0).T.astype(BF16))
    mixed = jnp.concatenate(mixed_pairs, axis=1)
    branch = dot(mixed, w_out[...]) + bias_row(raw_bias, "output", D)
    middle = x + gate1 * branch
    n2, inverse2 = normalize(middle)
    hidden2 = (n2 * (1.0 + scale2) + shift2).astype(BF16)

    b_up = bias_row(raw_bias, "up", FF)
    dfeed = (gate2 * g).astype(BF16)
    feed = jnp.zeros((S, D), F32)
    dhidden2 = jnp.zeros((S, D), F32)
    db_up = []
    hidden2_t = hidden2.T
    for c in range(4):
        lo = D * c
        upper = dot(hidden2, w_up[:, lo : lo + D]) + b_up[:, lo : lo + D]
        square = upper * upper
        t = jnp.tanh(0.7978845608028654 * (upper + 0.044715 * (upper * square)))
        half = 0.5 * (1.0 + t)
        activated = (upper * half).astype(BF16)
        slope = half + (0.5 * upper) * (1.0 - t * t) * (
            0.7978845608028654 * (1.0 + 0.134145 * square)
        )
        feed = feed + dot(activated, w_down[lo : lo + D, :])
        dupper = (dot(dfeed, w_down[lo : lo + D, :], 1, 1) * slope).astype(BF16)
        d_down[lo : lo + D, :] = dot(activated.T, dfeed).astype(BF16)
        d_up[:, lo : lo + D] = dot(hidden2_t, dupper).astype(BF16)
        db_up.append(total(dupper.astype(F32)))
        dhidden2 = dhidden2 + dot(dupper, w_up[:, lo : lo + D], 1, 1)
    feed = feed + bias_row(raw_bias, "down", D)
    result[0] = (middle + gate2 * feed).astype(BF16)
    dgate2 = total(g * feed)
    db_down = total(dfeed.astype(F32))
    dscale2, dshift2 = total(dhidden2 * n2), total(dhidden2)
    gmid = g + denormalize(dhidden2 * (1.0 + scale2), n2, inverse2)
    dgate1 = total(gmid * branch)
    dbranch = (gate1 * gmid).astype(BF16)
    d_out[...] = dot(mixed.T, dbranch).astype(BF16)
    db_out = total(dbranch.astype(F32))
    dmixed = dot(dbranch, w_out[...], 1, 1).astype(BF16)

    dq, dk, dv = [], [], []
    for i in range(3):
        q, v = pair(i, 0), pair(i, 2)
        dm = dmixed[:, 128 * i : 128 * i + 128]
        dq_t, dk_h, dv_h = [], [], []
        for h in range(2):
            probs = probs_ref[2 * i + h]
            dprobs = dot(v, jnp.where(halves[h], dm, nothing), 1, 1)
            dv_h.append(dot(probs.astype(BF16), dm))
            dscores = (probs * (dprobs - total(probs * dprobs))).astype(BF16)
            dk_h.append(dot(dscores, q))
            dq_t.append(dot(keys_t[i][64 * h : 64 * h + 64], dscores))
        dq.append((jnp.concatenate(dq_t, axis=0).T * FACTOR).astype(BF16))
        dk.append((jnp.where(halves[0], dk_h[0], dk_h[1]) * FACTOR).astype(BF16))
        dv.append(jnp.where(halves[0], dv_h[0], dv_h[1]).astype(BF16))
    dtriple = jnp.concatenate(dq + dk + dv, axis=1)
    d_att[...] = dot(hidden1.T, dtriple).astype(BF16)
    sums = total(dtriple.astype(F32))
    db_att = jnp.concatenate([sums[:, :D], sums[:, 2 * D :]], axis=1)
    dhidden1 = dot(dtriple, w_att[...], 1, 1)
    dscale1, dshift1 = total(dhidden1 * n1), total(dhidden1)
    token_grad[0] = gmid + denormalize(dhidden1 * (1.0 + scale1), n1, inverse1)

    dmod = jnp.concatenate([dshift1, dscale1, dgate1, dshift2, dscale2, dgate2], axis=1)
    dcact = jnp.zeros((D, 128), F32)
    for t in range(18):
        here = slice(128 * t, 128 * t + 128)
        dcact = dcact + w_mod[:, here].astype(F32) * dmod[:, here]
        d_mod[:, here] = (cact_column * dmod[:, here]).astype(BF16)
    condition_grad[...] = total(dcact.T) * (sigmoid * (1.0 + cond * (1.0 - sigmoid)))

    d_bias = (
        bias_block(dmod, "mod")
        + bias_block(db_att, "attend")
        + bias_block(db_out, "output")
        + bias_block(jnp.concatenate(db_up, axis=1), "up")
        + bias_block(db_down, "down")
    ).astype(BF16)
    rows, rows_down = spread_rows(True), spread_down(True)
    for group in range(8):
        here = slice(48 * group, 48 * group + 48)
        for p in range(PARTS):
            wide = WIDE if p < 2 else 128
            lo = WIDE * p
            if p == 0:
                mix = jnp.concatenate([d_up[here, 1152:1536], d_out[here, 0:128]], axis=1)
                last = jnp.concatenate(
                    [d_bias[16 * group : 16 * group + 16], jnp.zeros((16, 384), BF16)], axis=1
                )
            elif p == 1:
                mix = jnp.concatenate([d_out[here, 128:384], jnp.zeros((48, 256), BF16)], axis=1)
                last = jnp.zeros((16, wide), BF16)
            else:
                mix = jnp.zeros((48, wide), BF16)
                last = jnp.zeros((16, wide), BF16)
            laid = dot(
                rows,
                jnp.concatenate(
                    [
                        d_mod[here, lo : lo + wide],
                        d_mod[here, 1152 + lo : 1152 + lo + wide],
                        d_att[here, lo : lo + wide],
                        d_up[here, lo : lo + wide],
                        mix,
                        last,
                    ],
                    axis=0,
                ),
            ).astype(BF16)
            for m, s in enumerate(members(p, group)):
                packed[p, s, :, 0:wide] = laid[16 * m : 16 * m + 16]
            if p == 2:
                laid = dot(rows_down, d_down[192 * group : 192 * group + 192, :]).astype(BF16)
                for m, s in enumerate(members(p, group)):
                    packed[p, s, :, 128:512] = laid[16 * m : 16 * m + 16]


def reduce_kernel(
    packed, final,
    chip, ours, pass_on, turned, joined, ring, row, near, line, ends,
    send_c, recv_c, send1, recv1, send2, recv2, send3, recv3, send4, recv4,
):
    at, core = place()
    greet(at, core)

    def add(*blocks):
        out = blocks[0].astype(F32)
        for block in blocks[1:]:
            out = out + block.astype(F32)
        return out

    def chunk(p, by):
        return lax.rem(at[ORDERS[p][2]] + by, 4) * 16

    cross = {}
    for by in (2, 1, 3, 0):
        for p in range(PARTS):
            lo = chunk(p, by)
            cross[p, by] = remote(
                packed.at[p, pl.ds((1 - core) * 64 + lo, 16)],
                chip.at[p, pl.ds(lo, 16)],
                send_c.at[p, by],
                recv_c.at[p, by],
                device(at, 1 - core),
            )

    def to(p, by):
        return device(moved(at, ORDERS[p][2], by), core)

    waits = []
    for by in (2, 1, 3, 0):
        for p in range(PARTS):
            lo = chunk(p, by)
            cross[p, by].wait_recv()
            here = pl.ds(lo, 16)
            ours[p, here] = add(packed[p, pl.ds(core * 64 + lo, 16)], chip[p, here]).astype(BF16)
            if by == 2:
                for k in range(2):
                    waits.append(
                        remote(ours.at[p, pl.ds(lo + 8 * k, 8)], pass_on.at[p, k], send1.at[p, k], recv1.at[p, k], to(p, (1, 3)[k]))
                    )
            if by in (1, 3):
                k = (1, 3).index(by)
                waits.append(
                    remote(ours.at[p, pl.ds(lo + 8 * (1 - k), 8)], ring.at[p, k, pl.ds(8 * (1 - k), 8)], send1.at[p, 2 + k], recv1.at[p, 2 + k], to(p, by))
                )
    for p in range(PARTS):
        for k in range(2):
            waits[2 * p + k].wait_recv()
            lo = chunk(p, (1, 3)[k]) + 8 * k
            turned[p, k] = add(ours[p, pl.ds(lo, 8)], pass_on[p, k]).astype(BF16)
            waits.append(
                remote(turned.at[p, k], ring.at[p, k, pl.ds(8 * k, 8)], send2.at[p, k], recv2.at[p, k], to(p, (1, 3)[k]))
            )
    for p in range(PARTS):
        for k in range(2):
            waits[6 + 3 * k + p].wait_recv()
            waits[12 + 2 * p + k].wait_recv()
        joined[p] = add(ours[p, pl.ds(chunk(p, 0), 16)], ring[p, 0], ring[p, 1]).astype(BF16)
        b = ORDERS[p][1]
        for d in (2, 1, 3):
            waits.append(
                remote(joined.at[p, pl.ds(lax.rem(at[b] + d, 4) * 4, 4)], row.at[p, d - 1], send3.at[p, d - 1], recv3.at[p, d - 1], device(moved(at, b, d), core))
            )
    for p in range(PARTS):
        a, b, _ = ORDERS[p]
        for d in range(3):
            waits[18 + 3 * p + d].wait_recv()
        near[p] = add(joined[p, pl.ds(at[b] * 4, 4)], row[p, 0], row[p, 1], row[p, 2])
        line[p] = near[p].astype(BF16)
        for d in (2, 1, 3):
            waits.append(
                remote(line.at[p, pl.ds(lax.rem(at[a] + d, 4), 1)], ends.at[p, pl.ds(d - 1, 1)], send4.at[p, d - 1], recv4.at[p, d - 1], device(moved(at, a, d), core))
            )
    for p in range(PARTS):
        for d in range(3):
            waits[27 + 3 * p + d].wait_recv()
        final[:, WIDE * p : WIDE * p + WIDE] = add(near[p, at[ORDERS[p][0]]], ends[p, 0], ends[p, 1], ends[p, 2])
    for copy in [*cross.values(), *waits]:
        copy.wait_send()


def unpack_kernel(block, mod, b_mod, att, b_att, out, b_out, up, b_up, down, b_down):
    mod[0, :, 0:1152] = block[0:3, 0:1152]
    mod[0, :, 1152:2304] = block[3:6, 0:1152]
    att[0] = block[6:9, 0:1152]
    up[0, :, 0:1152] = block[9:12, 0:1152]
    up[0, :, 1152:1536] = block[12:15, 0:384]
    out[0] = block[12:15, 384:768]
    down[0] = block[0:12, 1152:1536]
    for ref, name in ((b_mod, "mod"), (b_att, "attend"), (b_out, "output"), (b_up, "up"), (b_down, "down")):
        size, lane = BIASES[name]
        ref[...] = block[15:16, lane : lane + size]


def whole(count):
    return [pl.BlockSpec(memory_space=pltpu.VMEM)] * count


def shape(*dims, dtype=BF16):
    return jax.ShapeDtypeStruct(dims, dtype)


def dma(*dims):
    return pltpu.SemaphoreType.DMA(dims)


def local(
    tokens, condition, modulation_weight, modulation_bias, attend_weight, attend_bias, output_weight, output_bias,
    up_weight, up_bias, down_weight, down_bias, cotangent,
):
    gathered = pl.pallas_call(
        gather_kernel,
        out_shape=[
            shape(D, 6 * D), shape(D, 3 * D), shape(D, D), shape(D, FF), shape(FF, D), shape(128, 128),
        ],
        in_specs=whole(10),
        out_specs=whole(6),
        scratch_shapes=[
            pltpu.VMEM((PARTS, 128, 16, WIDE), BF16),
            dma(PARTS, 3), dma(PARTS, 3), dma(PARTS, 3), dma(PARTS, 3), dma(PARTS, 2), dma(PARTS, 2),
            dma(PARTS, 2), dma(PARTS, 2), dma(PARTS, 5), dma(PARTS, 5),
        ],
        compiler_params=pltpu.CompilerParams(
            collective_id=0, has_side_effects=True, vmem_limit_bytes=VMEM_LIMIT
        ),
    )(
        modulation_weight, modulation_bias, attend_weight, attend_bias, output_weight, output_bias,
        up_weight, up_bias, down_weight, down_bias,
    )
    result, token_grad, condition_grad, packed = pl.pallas_call(
        block_kernel,
        out_shape=[
            shape(1, S, D), shape(1, S, D, dtype=F32), shape(1, D, dtype=F32), shape(PARTS, 128, 16, WIDE),
        ],
        in_specs=whole(9),
        out_specs=whole(4),
        scratch_shapes=[
            pltpu.VMEM((D, 6 * D), BF16), pltpu.VMEM((D, 3 * D), BF16), pltpu.VMEM((D, D), BF16),
            pltpu.VMEM((D, FF), BF16), pltpu.VMEM((FF, D), BF16), pltpu.VMEM((6, S, S), F32),
        ],
        compiler_params=pltpu.CompilerParams(vmem_limit_bytes=VMEM_LIMIT),
    )(tokens, condition, cotangent, *gathered)
    final = pl.pallas_call(
        reduce_kernel,
        out_shape=shape(16, 3 * WIDE, dtype=F32),
        in_specs=whole(1),
        out_specs=pl.BlockSpec(memory_space=pltpu.VMEM),
        scratch_shapes=[
            pltpu.VMEM((PARTS, 64, 16, WIDE), BF16),
            pltpu.VMEM((PARTS, 64, 16, WIDE), BF16),
            pltpu.VMEM((PARTS, 2, 8, 16, WIDE), BF16),
            pltpu.VMEM((PARTS, 2, 8, 16, WIDE), BF16),
            pltpu.VMEM((PARTS, 16, 16, WIDE), BF16),
            pltpu.VMEM((PARTS, 2, 16, 16, WIDE), BF16),
            pltpu.VMEM((PARTS, 3, 4, 16, WIDE), BF16),
            pltpu.VMEM((PARTS, 4, 16, WIDE), F32),
            pltpu.VMEM((PARTS, 4, 16, WIDE), BF16),
            pltpu.VMEM((PARTS, 3, 16, WIDE), BF16),
            dma(PARTS, 4), dma(PARTS, 4), dma(PARTS, 4), dma(PARTS, 4), dma(PARTS, 2), dma(PARTS, 2),
            dma(PARTS, 3), dma(PARTS, 3), dma(PARTS, 3), dma(PARTS, 3),
        ],
        compiler_params=pltpu.CompilerParams(
            collective_id=1, has_side_effects=True, vmem_limit_bytes=VMEM_LIMIT
        ),
    )(packed)
    grads = pl.pallas_call(
        unpack_kernel,
        out_shape=[
            shape(1, 3, 6 * D, dtype=F32), shape(1, 18, dtype=F32), shape(1, 3, 3 * D, dtype=F32),
            shape(1, 6, dtype=F32), shape(1, 3, D, dtype=F32), shape(1, 3, dtype=F32),
            shape(1, 3, FF, dtype=F32), shape(1, 12, dtype=F32), shape(1, 12, D, dtype=F32), shape(1, 3, dtype=F32),
        ],
        in_specs=whole(1),
        out_specs=whole(10),
    )(final)
    return (result, token_grad, condition_grad, *grads)


def solution(mesh):
    latents = P(("dp", "fsdp"), None, None)
    rows = P(None, ("dp", "fsdp"), None)
    entries = P(None, ("dp", "fsdp"))
    weights = (rows, entries) * 5
    return jax.shard_map(
        local,
        mesh=mesh,
        in_specs=(latents, P(("dp", "fsdp"), None), *weights, latents),
        out_specs=(latents, latents, P(("dp", "fsdp"), None), *weights),
        check_vma=False,
    )
```

time: 1150 us -> 92.1 us (0.08)
  blocking collectives: 771 us -> 0 us
  waiting for transfers between devices: 278 us -> 0 us
  Pallas kernels: 0 us -> 84.1 us
  local copies, waits for them, and re-layouts: 46.2 us -> 6.75 us
  matrix products: 23.4 us -> 0 us
  other arithmetic: 14.3 us -> 0 us
  between operations: 14.4 us -> 0.67 us
    all_gather x2 -> x0, blocking collectives: 635 us -> none  [the longest x1 323 us: fetch_forward(): lax.all_gather(shards[2][layer_index], ('dp', 'fsdp'), axis=0, tiled=True)]
    all_gather x3 -> x0, waiting for transfers between devices: 187 us -> none  [the longest x1 187 us: fetch_forward(): lax.all_gather(shards[8][layer_index], ('dp', 'fsdp'), axis=0, tiled=True)]
    unnamed x2 -> x0, blocking collectives: 135 us -> none
    unnamed x5 -> x0, waiting for transfers between devices: 90.1 us -> none
    pallas_call x0 -> x4, Pallas kernels: none -> 84.1 us  [the longest x1 36.1 us: local(): pl.pallas_call(gather_kernel, out_shape=[shape(D, 6 * D), shape(D, 3 * D)...]
    dot_general x21 -> x0, matrix products: 23.4 us -> none  [the longest x5 10.4 us: product(): return jnp.dot(left, right, preferred_element_type=jnp.float32)]
    scatter-add x9 -> x0, local copies, waits for them, and re-layouts: 21.3 us -> none  [local(): accumulated[member].at[layer_index].add(layer_grads[member])]
    unnamed x131 -> x5, local copies, waits for them, and re-layouts: 23.2 us -> 6.75 us
  transfers between devices with their start and end apart: 4 -> 0, of which waited for: 2 -> 0; matrix products, arithmetic and copies ran while one was open for 3% -> 0% of each run, Pallas kernels for 0% -> 0%
where the time goes in v1:
time: 92.1 us; the launch traced here: 91.5 us
  Pallas kernels  84.1 us (91%)
  local copies, waits for them, and re-layouts  6.75 us (7%)
    pallas_call x1, Pallas kernels, local(): pl.pallas_call(gather_kernel, out_shape=[shape(D, 6 * D), shape(D, 3 * D)...  36.1 us
    pallas_call x1, Pallas kernels, local(): pl.pallas_call(reduce_kernel, out_shape=shape(16, 3 * WIDE, dtype=F32), i...  27.5 us
    pallas_call x1, Pallas kernels, local(): pl.pallas_call(block_kernel, out_shape=[shape(1, S, D), shape(1, S, D, dt...  19 us
    unnamed x5, local copies, waits for them, and re-layouts  6.75 us

profile of v1, /device:TPU:1, one launch (start us, length us, event | category | flops | bytes accessed | tf_op | source)
XLA Modules:
  0.0 91.5 jit_solution(6123656008366318853)
XLA Ops:
  0.6 36.1 %shard_map.228 = (bf16[384,2304]{1,0:T(8,128)(2,1)}, bf16[384,1152]{1,0:T(8,128)(2,1)}, bf16[384,384]{1,0:T(8,128)(2,1)}, bf16[384,1536]{1,0:T(8,128)(2,1)}, bf1...) custom-call(bf16[1,3,2304]{2,1,0:T(4,128)(2,1)} %mod.1, bf16[1,18]{1,0:T(2,128)(2,1)} %b_mod.1, bf16[1,3,1152]{2,1,0:T(4,128)(2,1)} %att.1, ...), custom_call_target="tpu_custom_call" | custom-call | tf_op jit(solution)/shard_map/pallas_call | solution.py:534
  36.8 19.0 %shard_map.229 = (bf16[1,256,384]{2,1,0:T(8,128)(2,1)}, f32[1,256,384]{2,1,0:T(8,128)}, f32[1,384]{1,0:T(1,128)}, bf16[3,128,16,512]{3,2,1,0:T(8,128)(2,1)}) custom-call(bf16[1,256,384]{2,1,0:T(8,128)(2,1)} %tokens.1, bf16[1,384]{1,0:T(2,128)(2,1)} %condition.1, bf16[1,256,384]{2,1,0:T(8,128)(2,1)} %cotangent.1, bf16[384,2304]{1,0:T(8,128)(2,1)} %get-tuple-element.33.w_mod, ...), custom_call_target="tpu_custom_call" | custom-call | tf_op jit(solution)/shard_map/pallas_call | solution.py:553
  55.7 27.5 %shard_map.230.block = f32[16,1536]{1,0:T(8,128)} custom-call(bf16[3,128,16,512]{3,2,1,0:T(8,128)(2,1)} %get-tuple-element.42.packed), custom_call_target="tpu_custom_call" | custom-call | tf_op jit(solution)/shard_map/pallas_call | solution.py:566
  83.2 1.6 %shard_map.231 = (f32[1,3,2304]{2,1,0:T(4,128)}, f32[1,18]{1,0:T(1,128)}, f32[1,3,1152]{2,1,0:T(4,128)}, f32[1,6]{1,0:T(1,128)}, f32[1,3,384]{2,1,0:T(4,128)}, /...) custom-call(f32[16,1536]{1,0:T(8,128)} %shard_map.230.block), custom_call_target="tpu_custom_call" | custom-call | tf_op jit(solution)/shard_map/pallas_call | solution.py:589
  84.8 1.4 %copy.26 = f32[1,3,2304]{2,0,1:T(1,128)} copy(f32[1,3,2304]{2,1,0:T(4,128)} %get-tuple-element.56) | data formatting | bytes 55296
  86.2 1.3 %copy.28 = f32[1,3,384]{2,0,1:T(1,128)} copy(f32[1,3,384]{2,1,0:T(4,128)} %get-tuple-element.60) | data formatting | bytes 9216
  87.5 1.3 %copy.27 = f32[1,3,1152]{2,0,1:T(1,128)} copy(f32[1,3,1152]{2,1,0:T(4,128)} %get-tuple-element.58) | data formatting | bytes 27648
  88.8 1.4 %copy.29 = f32[1,3,1536]{2,0,1:T(1,128)} copy(f32[1,3,1536]{2,1,0:T(4,128)} %get-tuple-element.62) | data formatting | bytes 36864
  90.2 1.4 %copy.30 = f32[1,12,384]{2,0,1:T(1,128)} copy(f32[1,12,384]{2,1,0:T(8,128)} %get-tuple-element.64) | data formatting | bytes 36864

commit v2 on v1

v2 whole, which is shorter than its diff:
```python
import jax
import jax.numpy as jnp
from jax import lax
from jax.experimental import pallas as pl
from jax.experimental.pallas import tpu as pltpu
from jax.sharding import PartitionSpec as P

MESH = pl.DeviceIdType.MESH
F32 = jnp.float32
BF16 = jnp.bfloat16
EPS = 1e-06
HEAD = 64
D = 384
FF = 1536
S = 256
FACTOR = HEAD ** (-0.5)
VMEM_LIMIT = 60 * 1024 * 1024

PARTS = 3
ORDERS = ((0, 1, 2), (1, 2, 0), (2, 0, 1))
BIASES = {"mod": (18, 0, 0), "attend": (6, 18, 0), "output": (3, 24, 6), "up": (12, 27, 9), "down": (3, 39, 21)}


def dot(a, b, ca=1, cb=0):
    return lax.dot_general(a, b, (((ca,), (cb,)), ((), ())), preferred_element_type=F32)


def place():
    dp, fsdp = lax.axis_index("dp"), lax.axis_index("fsdp")
    core = lax.rem(dp, 2)
    y = lax.rem(lax.div(dp, 2), 4)
    x = lax.rem(lax.div(dp, 8), 2) + 2 * fsdp
    return (x, y, lax.div(dp, 16)), core


def device(at, core):
    x, y, z = at
    return (z * 16 + lax.rem(x, 2) * 8 + y * 2 + core, lax.div(x, 2))


def moved(at, axis, by):
    return tuple(lax.rem(c + by, 4) if i == axis else c for i, c in enumerate(at))


def slot_of(part, x, y, z, core):
    at = (x, y, z)
    a, b, c = ORDERS[part]
    return ((core * 4 + at[c]) * 4 + at[b]) * 4 + at[a]


def announce(at, core):
    barrier = pltpu.get_barrier_semaphore()
    for axis in range(3):
        for by in range(1, 4):
            pl.semaphore_signal(
                barrier, inc=1, device_id=device(moved(at, axis, by), core), device_id_type=MESH
            )
    pl.semaphore_signal(barrier, inc=1, device_id=device(at, 1 - core), device_id_type=MESH)


class Moves:
    def __init__(self, at, core, send, recv):
        self.at, self.core, self.send, self.recv = at, core, send, recv
        self.copies = {}

    def start(self, stage, p, k, src, dst, axis, by):
        to = device(self.at, 1 - self.core) if axis is None else device(moved(self.at, axis, by), self.core)
        copy = pltpu.make_async_remote_copy(
            src_ref=src, dst_ref=dst, send_sem=self.send.at[stage, p, k], recv_sem=self.recv.at[stage, p, k],
            device_id=to, device_id_type=MESH,
        )
        copy.start()
        self.copies[stage, p, k] = copy

    def arrived(self, stage, p, ks):
        for k in ks:
            self.copies[stage, p, k].wait_recv()

    def sent(self):
        for copy in self.copies.values():
            copy.wait_send()


class Gather(Moves):
    def __init__(self, at, core, held, send, recv):
        super().__init__(at, core, send, recv)
        self.held = held

    def own(self, p):
        return slot_of(p, *self.at, self.core)

    def first(self, p):
        block = self.held.at[p, pl.ds(self.own(p), 1)]
        for d in (1, 3, 2):
            self.start(0, p, d, block, block, ORDERS[p][0], d)

    def second(self, p):
        self.arrived(0, p, (1, 3, 2))
        _, b, c = ORDERS[p]
        block = self.held.at[p, pl.ds(((self.core * 4 + self.at[c]) * 4 + self.at[b]) * 4, 4)]
        for d in (1, 3, 2):
            self.start(1, p, d, block, block, b, d)

    def plane(self, p, by):
        lo = (self.core * 4 + lax.rem(self.at[ORDERS[p][2]] + by, 4)) * 16
        return self.held.at[p, pl.ds(lo, 16)]

    def third(self, p):
        self.arrived(1, p, (1, 3, 2))
        block = self.plane(p, 0)
        for d in (1, 3, 2):
            self.start(2, p, d, block, block, ORDERS[p][2], d)
        self.start(3, p, 0, block, block, None, 0)

    def across(self, p, d):
        self.arrived(2, p, (d,))
        block = self.plane(p, 4 - d)
        self.start(3, p, d, block, block, None, 0)

    def complete(self, p):
        self.arrived(3, p, range(4))


def add(*blocks):
    out = blocks[0].astype(F32)
    for block in blocks[1:]:
        out = out + block.astype(F32)
    return out


class Reduce(Moves):
    def __init__(self, at, core, packed, chip, ours, ring, joined, row, near, line, ends, send, recv):
        super().__init__(at, core, send, recv)
        self.packed, self.chip, self.ours, self.ring, self.joined = packed, chip, ours, ring, joined
        self.row, self.near, self.line, self.ends = row, near, line, ends

    def chunk(self, p, by):
        return lax.rem(self.at[ORDERS[p][2]] + by, 4) * 16

    def across(self, p):
        for by in (2, 1, 3, 0):
            lo = self.chunk(p, by)
            src = self.packed.at[p, pl.ds((1 - self.core) * 64 + lo, 16)]
            self.start(0, p, by, src, self.chip.at[p, pl.ds(lo, 16)], None, 0)

    def third(self, p):
        for by in (2, 1, 3, 0):
            lo = self.chunk(p, by)
            here = pl.ds(lo, 16)
            self.arrived(0, p, (by,))
            self.ours[p, here] = add(self.packed[p, pl.ds(self.core * 64 + lo, 16)], self.chip[p, here]).astype(BF16)
            if by:
                self.start(1, p, by, self.ours.at[p, here], self.ring.at[p, by - 1], ORDERS[p][2], by)

    def second(self, p):
        self.arrived(1, p, (1, 3, 2))
        ring = self.ring
        self.joined[p] = add(self.ours[p, pl.ds(self.chunk(p, 0), 16)], ring[p, 0], ring[p, 1], ring[p, 2]).astype(BF16)
        b = ORDERS[p][1]
        for d in (2, 1, 3):
            src = self.joined.at[p, pl.ds(lax.rem(self.at[b] + d, 4) * 4, 4)]
            self.start(2, p, d, src, self.row.at[p, d - 1], b, d)

    def first(self, p):
        self.arrived(2, p, (1, 3, 2))
        a, b, _ = ORDERS[p]
        row = self.row
        self.near[p] = add(self.joined[p, pl.ds(self.at[b] * 4, 4)], row[p, 0], row[p, 1], row[p, 2])
        self.line[p] = self.near[p].astype(BF16)
        for d in (2, 1, 3):
            src = self.line.at[p, pl.ds(lax.rem(self.at[a] + d, 4), 1)]
            self.start(3, p, d, src, self.ends.at[p, pl.ds(d - 1, 1)], a, d)

    def total(self, p):
        self.arrived(3, p, (1, 3, 2))
        ends = self.ends
        return add(self.near[p, self.at[ORDERS[p][0]]], ends[p, 0], ends[p, 1], ends[p, 2])


def spread(place_of, count, transposed):
    shape = (256, count) if transposed else (count, 256)
    n = lax.broadcasted_iota(jnp.int32, shape, 0 if transposed else 1)
    o = lax.broadcasted_iota(jnp.int32, shape, 1 if transposed else 0)
    return jnp.where(place_of(n >> 4, n & 15) == o, 1.0, 0.0).astype(BF16)


def threes(member, row):
    section = (row * 11) >> 5
    return section * 48 + member * 3 + (row - 3 * section)


def place_first(member, row):
    return jnp.where(row == 15, 240 + member, threes(member, row))


def place_up(member, row):
    return jnp.where(row < 6, threes(member, row), -1)


def place_left(member, row):
    return jnp.where((row >= 6) & (row < 12), member * 12 + row - 6, -1)


def place_right(member, row):
    return jnp.where((row >= 6) & (row < 12), member * 12 + row, -1)


def place_back(member, row):
    return jnp.where(row < 6, threes(member, row), jnp.where((row >= 12) & (row < 15), threes(member, row) - 96, -1))


def place_attend(member, row):
    return jnp.where(row < 9, threes(member, row), jnp.where(row == 9, 144 + member, -1))


def members(part, group):
    z, x_lo = group // 2, group % 2
    return [
        slot_of(part, 2 * x_hi + x_lo, y, z, core)
        for y in range(4)
        for core in range(2)
        for x_hi in range(2)
    ]


def bias_map(name, count, lane):
    size = BIASES[name][0]
    n = lax.broadcasted_iota(jnp.int32, (128, count), 1)
    owner = (n * -(-65536 // size)) >> 16
    k = lax.broadcasted_iota(jnp.int32, (128, count), 0)
    return owner == k, (n - owner * size + lane) == k


def bias_row(bias, name, count):
    mine, lane = bias_map(name, count, BIASES[name][1])
    picked = dot(bias, jnp.where(lane, 1.0, 0.0).astype(BF16))
    return jnp.sum(jnp.where(mine, picked, 0.0), axis=0, keepdims=True)


def bias_block(row, name):
    mine, lane = bias_map(name, row.shape[1], BIASES[name][2])
    placed = jnp.where(mine, row, 0.0).astype(BF16)
    return dot(placed, jnp.where(lane, 1.0, 0.0).astype(BF16), 1, 1)


def normalize(v):
    shifted = v - jnp.mean(v, axis=-1, keepdims=True)
    inverse = lax.rsqrt(jnp.mean(shifted * shifted, axis=-1, keepdims=True) + EPS)
    return shifted * inverse, inverse


def denormalize(e, n, inverse):
    return inverse * (
        e - jnp.mean(e, axis=-1, keepdims=True) - n * jnp.mean(e * n, axis=-1, keepdims=True)
    )


def total(v):
    return jnp.sum(v, axis=0, keepdims=True)


def block_kernel(
    tokens, condition, mod, b_mod, att, b_att, out, b_out, up, b_up, down, b_down, cotangent,
    result, token_grad, condition_grad, grad_ff, grad_att, grad_mod,
    held1, held2, held3, w_mod, w_att, w_out, w_up, w_down, bias, cact_all,
    d_att, d_out, d_up, d_down, probs_ref,
    packed, chip, ours, ring, joined, row, near, line, ends,
    packed_a, chip_a, ours_a, ring_a, joined_a, row_a, near_a, line_a, ends_a,
    sems,
):
    at, core = place()
    announce(at, core)
    first, second, third = [
        Gather(at, core, held, sems.at[i, 0], sems.at[i, 1]) for i, held in enumerate((held1, held2, held3))
    ]
    back = Reduce(at, core, packed, chip, ours, ring, joined, row, near, line, ends, sems.at[3, 0], sems.at[3, 1])
    last = Reduce(
        at, core, packed_a, chip_a, ours_a, ring_a, joined_a, row_a, near_a, line_a, ends_a, sems.at[4, 0], sems.at[4, 1]
    )

    def load(ref, lo, hi):
        return ref[0, :, lo:hi].astype(F32)

    cond = condition[...].astype(F32)
    sigmoid = 1.0 / (1.0 + jnp.exp(-cond))
    cact = (cond * sigmoid).astype(BF16).astype(F32)
    bias_line = jnp.concatenate(
        [ref[...].astype(F32) for ref in (b_mod, b_att, b_out, b_up, b_down)]
        + [jnp.zeros((1, 128 - 42), F32), cact, jnp.zeros((1, 256), F32)],
        axis=1,
    )
    mine = jnp.concatenate(
        [load(mod, 0, 768), load(mod, 768, 1536), load(mod, 1536, 2304), load(att, 0, 768),
         jnp.concatenate([load(att, 768, 1152), load(out, 0, 384)], axis=1), bias_line],
        axis=0,
    ).astype(BF16)
    tall = down[0].astype(F32)
    mine2 = jnp.concatenate(
        [load(up, 0, 768), load(up, 768, 1536), jnp.concatenate([tall[0:6], tall[6:12]], axis=1), jnp.zeros((4, 768), F32)],
        axis=0,
    ).astype(BF16)
    for p in range(PARTS):
        held1[p, first.own(p)] = mine[:, 256 * p : 256 * p + 256]
        held2[p, second.own(p)] = mine2[:, 256 * p : 256 * p + 256]

    pl.semaphore_wait(pltpu.get_barrier_semaphore(), 10)
    for p in range(PARTS):
        first.first(p)
    for p in range(PARTS):
        second.first(p)

    x = tokens[0].astype(F32)
    g = cotangent[0].astype(F32)
    cact_column = jnp.broadcast_to(cact, (128, D)).T
    n1, inverse1 = normalize(x)

    for p in range(PARTS):
        first.second(p)
    for p in range(PARTS):
        second.second(p)
    for p in range(PARTS):
        first.third(p)
    for p in range(PARTS):
        second.third(p)
    for d in (1, 3, 2):
        for p in range(PARTS):
            first.across(p, d)

    rows = spread(place_first, 256, False)
    for p in range(PARTS):
        first.complete(p)
        lo = 256 * p
        for group in range(8):
            here = slice(48 * group, 48 * group + 48)
            few = slice(16 * group, 16 * group + 16)
            laid = dot(rows, jnp.concatenate([held1[p, s] for s in members(p, group)], axis=0)).astype(BF16)
            for i in range(3):
                w_mod[here, 768 * i + lo : 768 * i + lo + 256] = laid[48 * i : 48 * i + 48]
            w_att[here, lo : lo + 256] = laid[144:192]
            if p == 0:
                w_att[here, 768:1024] = laid[192:240]
                bias[few, :] = laid[240:256, 0:128]
                cact_all[few, 0:128] = laid[240:256, 128:256]
            elif p == 1:
                w_att[here, 1024:1152] = laid[192:240, 0:128]
                w_out[here, 0:128] = laid[192:240, 128:256]
                cact_all[few, 128:384] = laid[240:256]
            else:
                w_out[here, 128:384] = laid[192:240]

    raw_bias = bias[...]
    modulation = jnp.concatenate(
        [total(w_mod[:, 128 * t : 128 * t + 128].astype(F32) * cact_column) for t in range(18)],
        axis=1,
    ) + bias_row(raw_bias, "mod", 6 * D)
    shift1, scale1, gate1, shift2, scale2, gate2 = [
        modulation[:, D * i : D * i + D] for i in range(6)
    ]
    hidden1 = (n1 * (1.0 + scale1) + shift1).astype(BF16)
    b_attend = bias_row(raw_bias, "attend", 2 * D)
    b_full = jnp.concatenate([b_attend[:, :D], jnp.zeros((1, D), F32), b_attend[:, D:]], axis=1)
    triple = (dot(hidden1, w_att[...]) + b_full).astype(BF16)

    def pair(i, which):
        lo = D * which + 128 * i
        return triple[:, lo : lo + 128]

    for d in (1, 3, 2):
        for p in range(PARTS):
            second.across(p, d)

    lane = lax.broadcasted_iota(jnp.int32, (S, 128), 1)
    halves = [lane < 64, lane >= 64]
    nothing = jnp.zeros((S, 128), BF16)
    mixed_pairs = []
    keys_t = []
    for i in range(3):
        q, k, v = pair(i, 0), pair(i, 1), pair(i, 2)
        v_t = v.T
        keys_t.append(k.T)
        mixed_t = []
        for h in range(2):
            scores = dot(k, jnp.where(halves[h], q, nothing), 1, 1) * FACTOR
            e = jnp.exp(scores - jnp.max(scores, axis=0, keepdims=True))
            probs = e * (1.0 / total(e))
            probs_ref[2 * i + h] = probs
            mixed_t.append(dot(v_t[64 * h : 64 * h + 64], probs.astype(BF16)))
        mixed_pairs.append(jnp.concatenate(mixed_t, axis=0).T.astype(BF16))
    mixed = jnp.concatenate(mixed_pairs, axis=1)
    branch = dot(mixed, w_out[...]) + bias_row(raw_bias, "output", D)
    middle = x + gate1 * branch
    n2, inverse2 = normalize(middle)
    hidden2 = (n2 * (1.0 + scale2) + shift2).astype(BF16)

    rows = spread(place_up, 96, False)
    left, right = spread(place_left, 192, False), spread(place_right, 192, False)
    for p in range(PARTS):
        second.complete(p)
    for group in range(8):
        here = slice(48 * group, 48 * group + 48)
        blocks = [jnp.concatenate([held2[p, s] for s in members(p, group)], axis=0) for p in range(PARTS)]
        for p in range(PARTS):
            laid = dot(rows, blocks[p]).astype(BF16)
            w_up[here, 256 * p : 256 * p + 256] = laid[0:48]
            w_up[here, 768 + 256 * p : 1024 + 256 * p] = laid[48:96]
        low = dot(left, jnp.concatenate([blocks[0], blocks[1][:, :128]], axis=1))
        high = dot(right, jnp.concatenate([blocks[1][:, 128:], blocks[2]], axis=1))
        w_down[192 * group : 192 * group + 192, :] = (low + high).astype(BF16)

    b_upper = bias_row(raw_bias, "up", FF)
    dfeed = (gate2 * g).astype(BF16)
    feed = jnp.zeros((S, D), F32)
    dhidden2 = jnp.zeros((S, D), F32)
    db_up = []
    hidden2_t = hidden2.T
    for c in range(4):
        lo = D * c
        upper = dot(hidden2, w_up[:, lo : lo + D]) + b_upper[:, lo : lo + D]
        square = upper * upper
        t = jnp.tanh(0.7978845608028654 * (upper + 0.044715 * (upper * square)))
        half = 0.5 * (1.0 + t)
        activated = (upper * half).astype(BF16)
        slope = half + (0.5 * upper) * (1.0 - t * t) * (
            0.7978845608028654 * (1.0 + 0.134145 * square)
        )
        feed = feed + dot(activated, w_down[lo : lo + D, :])
        dupper = (dot(dfeed, w_down[lo : lo + D, :], 1, 1) * slope).astype(BF16)
        d_down[lo : lo + D, :] = dot(activated.T, dfeed).astype(BF16)
        d_up[:, lo : lo + D] = dot(hidden2_t, dupper).astype(BF16)
        db_up.append(total(dupper.astype(F32)))
        dhidden2 = dhidden2 + dot(dupper, w_up[:, lo : lo + D], 1, 1)
    feed = feed + bias_row(raw_bias, "down", D)
    result[0] = (middle + gate2 * feed).astype(BF16)
    dgate2 = total(g * feed)
    db_down = total(dfeed.astype(F32))
    dscale2, dshift2 = total(dhidden2 * n2), total(dhidden2)
    gmid = g + denormalize(dhidden2 * (1.0 + scale2), n2, inverse2)
    dgate1 = total(gmid * branch)
    dbranch = (gate1 * gmid).astype(BF16)
    d_out[...] = dot(mixed.T, dbranch).astype(BF16)
    db_out = total(dbranch.astype(F32))

    rows = spread(place_back, 144, True)
    left, right = spread(place_left, 192, True), spread(place_right, 192, True)
    for p in range(PARTS):
        for group in range(8):
            here = slice(48 * group, 48 * group + 48)
            tall = slice(192 * group, 192 * group + 192)
            if p == 0:
                extra = d_out[here, 0:256]
                stretched = dot(left, d_down[tall, 0:256])
            elif p == 1:
                extra = jnp.concatenate([d_out[here, 256:384], jnp.zeros((48, 128), BF16)], axis=1)
                stretched = jnp.concatenate([dot(left, d_down[tall, 256:384]), dot(right, d_down[tall, 0:128])], axis=1)
            else:
                extra = jnp.zeros((48, 256), BF16)
                stretched = dot(right, d_down[tall, 128:384])
            flat = jnp.concatenate(
                [d_up[here, 256 * p : 256 * p + 256], d_up[here, 768 + 256 * p : 1024 + 256 * p], extra], axis=0
            )
            laid = (dot(rows, flat) + stretched).astype(BF16)
            for m, s in enumerate(members(p, group)):
                packed[p, s] = laid[16 * m : 16 * m + 16]
        back.across(p)

    dmixed = dot(dbranch, w_out[...], 1, 1).astype(BF16)

    dq, dk, dv = [], [], []
    for i in range(3):
        q, v = pair(i, 0), pair(i, 2)
        dm = dmixed[:, 128 * i : 128 * i + 128]
        dq_t, dk_h, dv_h = [], [], []
        for h in range(2):
            probs = probs_ref[2 * i + h]
            dprobs = dot(v, jnp.where(halves[h], dm, nothing), 1, 1)
            dv_h.append(dot(probs.astype(BF16), dm))
            dscores = (probs * (dprobs - total(probs * dprobs))).astype(BF16)
            dk_h.append(dot(dscores, q))
            dq_t.append(dot(keys_t[i][64 * h : 64 * h + 64], dscores))
        dq.append((jnp.concatenate(dq_t, axis=0).T * FACTOR).astype(BF16))
        dk.append((jnp.where(halves[0], dk_h[0], dk_h[1]) * FACTOR).astype(BF16))
        dv.append(jnp.where(halves[0], dv_h[0], dv_h[1]).astype(BF16))
        back.third(i)
    dtriple = jnp.concatenate(dq + dk + dv, axis=1)
    d_att[...] = dot(hidden1.T, dtriple).astype(BF16)
    sums = total(dtriple.astype(F32))
    db_att = jnp.concatenate([sums[:, :D], sums[:, 2 * D :]], axis=1)
    d_bias = (
        bias_block(db_att, "attend")
        + bias_block(db_out, "output")
        + bias_block(jnp.concatenate(db_up, axis=1), "up")
        + bias_block(db_down, "down")
    ).astype(BF16)
    rows = spread(place_attend, 160, True)
    for group in range(8):
        here = slice(48 * group, 48 * group + 48)
        biases = jnp.concatenate([d_bias[16 * group : 16 * group + 16], jnp.zeros((16, 256), BF16)], axis=1)
        flat = jnp.concatenate([d_att[here, 0:384], d_att[here, 384:768], d_att[here, 768:1152], biases], axis=0)
        laid = dot(rows, flat).astype(BF16)
        for p in range(PARTS):
            for m, s in enumerate(members(p, group)):
                packed_a[p, s] = laid[16 * m : 16 * m + 16, 128 * p : 128 * p + 128]
    for p in range(PARTS):
        last.across(p)

    dhidden1 = dot(dtriple, w_att[...], 1, 1)
    dscale1, dshift1 = total(dhidden1 * n1), total(dhidden1)
    dmods = [dshift1, dscale1, dgate1, dshift2, dscale2, dgate2]
    vectors = jnp.concatenate(dmods + [jnp.zeros((2, D), F32)], axis=0)
    for p in range(PARTS):
        held3[p, third.own(p)] = vectors[:, 128 * p : 128 * p + 128]
        third.first(p)
    for p in range(PARTS):
        last.third(p)
    for p in range(PARTS):
        back.second(p)
    token_grad[0] = gmid + denormalize(dhidden1 * (1.0 + scale1), n1, inverse1)
    for p in range(PARTS):
        third.second(p)

    dmod = jnp.concatenate(dmods, axis=1)
    dcact = jnp.zeros((D, 128), F32)
    for t in range(18):
        here = slice(128 * t, 128 * t + 128)
        dcact = dcact + w_mod[:, here].astype(F32) * dmod[:, here]
    condition_grad[...] = total(dcact.T) * (sigmoid * (1.0 + cond * (1.0 - sigmoid)))

    for p in range(PARTS):
        last.second(p)
    for p in range(PARTS):
        back.first(p)
    for p in range(PARTS):
        third.third(p)

    index = 2 * lax.axis_index("dp") + lax.axis_index("fsdp")
    feature = lax.broadcasted_iota(jnp.int32, (8, D), 1)
    r = lax.broadcasted_iota(jnp.int32, (8, D), 0)
    pick = jnp.where((feature == 3 * index + r) & (r < 3), 1.0, 0.0).astype(BF16)
    columns = dot(pick, cact_all[...], 1, 1).astype(BF16)
    natural = lax.broadcasted_iota(jnp.int32, (128, 1024), 0)
    j = lax.broadcasted_iota(jnp.int32, (128, 1024), 1) >> 3
    stacked = lax.broadcasted_iota(jnp.int32, (64, 1024), 0)
    inner = lax.broadcasted_iota(jnp.int32, (64, 1024), 1) & 7
    weighing = []
    for p in range(PARTS):
        a, b, c = ORDERS[p]
        coordinate = {c: (j >> 4) & 3, b: (j >> 2) & 3, a: j & 3}
        xj, yj, zj = coordinate[0], coordinate[1], coordinate[2]
        source = zj * 32 + (xj & 1) * 16 + yj * 4 + (j >> 6) * 2 + (xj >> 1)
        expanded = dot(columns, jnp.where(source == natural, 1.0, 0.0).astype(BF16))
        tiled = jnp.concatenate([expanded] * 8, axis=0)
        tiled = jnp.where((stacked & 7) == 3, 1.0, tiled)
        weighing.append(jnp.where((stacked >> 3) == inner, tiled, 0.0).astype(BF16))

    for p in range(PARTS):
        last.first(p)
    for p in range(PARTS):
        grad_ff[:, 256 * p : 256 * p + 256] = back.total(p)
    for d in (1, 3, 2):
        for p in range(PARTS):
            third.across(p, d)
    for p in range(PARTS):
        grad_att[:, 128 * p : 128 * p + 128] = last.total(p)
    weighed = []
    for p in range(PARTS):
        third.complete(p)
        weighed.append(dot(weighing[p], held3[p].reshape(1024, 128).astype(BF16)))
    grads = jnp.concatenate(
        [weighed[p][8 * i : 8 * i + 8] for i in range(6) for p in range(PARTS)], axis=1
    )
    n = lax.broadcasted_iota(jnp.int32, (6 * D, 128), 0)
    k = lax.broadcasted_iota(jnp.int32, (6 * D, 128), 1)
    mine = jnp.where((n == 18 * index + k) & (k < 18), 1.0, 0.0).astype(BF16)
    grad_mod[:, 0 : 6 * D] = grads
    grad_mod[:, 6 * D :] = dot(grads.astype(BF16), mine)
    for moves in (first, second, third, back, last):
        moves.sent()


def unpack_kernel(
    result_in, token_in, condition_in, ff, attend, modulation,
    result, token_grad, condition_grad, mod, b_mod, att, b_att, out, b_out, up, b_up, down, b_down,
):
    result[...] = result_in[...]
    token_grad[...] = token_in[...]
    condition_grad[...] = condition_in[...]
    mod[:, 0, :] = modulation[0:3, 0 : 6 * D]
    b_mod[...] = modulation[3:4, 6 * D : 6 * D + 18]
    for i in range(3):
        att[:, 0, D * i : D * i + D] = attend[3 * i : 3 * i + 3, :]
    for i in range(2):
        up[:, 0, 768 * i : 768 * i + 768] = ff[3 * i : 3 * i + 3, :]
        down[6 * i : 6 * i + 6, 0, :] = ff[6:12, D * i : D * i + D]
    out[:, 0, :] = ff[12:15, 0:D]
    for ref, name in ((b_att, "attend"), (b_out, "output"), (b_up, "up"), (b_down, "down")):
        size, _, lane = BIASES[name]
        ref[...] = attend[9:10, lane : lane + size]


def whole(count):
    return [pl.BlockSpec(memory_space=pltpu.VMEM)] * count


def shape(*dims, dtype=BF16):
    return jax.ShapeDtypeStruct(dims, dtype)


def reduce_scratch(wide):
    return [
        pltpu.VMEM((PARTS, 128, 16, wide), BF16),
        pltpu.VMEM((PARTS, 64, 16, wide), BF16),
        pltpu.VMEM((PARTS, 64, 16, wide), BF16),
        pltpu.VMEM((PARTS, 3, 16, 16, wide), BF16),
        pltpu.VMEM((PARTS, 16, 16, wide), BF16),
        pltpu.VMEM((PARTS, 3, 4, 16, wide), BF16),
        pltpu.VMEM((PARTS, 4, 16, wide), F32),
        pltpu.VMEM((PARTS, 4, 16, wide), BF16),
        pltpu.VMEM((PARTS, 3, 16, wide), BF16),
    ]


def local(*args):
    outs = [
        shape(1, S, D), shape(1, S, D, dtype=F32), shape(1, D, dtype=F32),
    ]
    computed = pl.pallas_call(
        block_kernel,
        out_shape=outs + [shape(16, 768, dtype=F32), shape(16, D, dtype=F32), shape(8, 6 * D + 128, dtype=F32)],
        in_specs=whole(13),
        out_specs=whole(6),
        scratch_shapes=[
            pltpu.VMEM((PARTS, 128, 16, 256), BF16),
            pltpu.VMEM((PARTS, 128, 16, 256), BF16),
            pltpu.VMEM((PARTS, 128, 8, 128), F32),
            pltpu.VMEM((D, 6 * D), BF16), pltpu.VMEM((D, 3 * D), BF16), pltpu.VMEM((D, D), BF16),
            pltpu.VMEM((D, FF), BF16), pltpu.VMEM((FF, D), BF16), pltpu.VMEM((128, 128), BF16), pltpu.VMEM((128, D), BF16),
            pltpu.VMEM((D, 3 * D), BF16), pltpu.VMEM((D, D), BF16),
            pltpu.VMEM((D, FF), BF16), pltpu.VMEM((FF, D), BF16), pltpu.VMEM((6, S, S), F32),
            *reduce_scratch(256),
            *reduce_scratch(128),
            pltpu.SemaphoreType.DMA((5, 2, 4, PARTS, 4)),
        ],
        compiler_params=pltpu.CompilerParams(
            collective_id=0, has_side_effects=True, vmem_limit_bytes=VMEM_LIMIT
        ),
    )(*args)
    grads = [
        shape(3, 1, 6 * D, dtype=F32), shape(1, 18, dtype=F32), shape(3, 1, 3 * D, dtype=F32),
        shape(1, 6, dtype=F32), shape(3, 1, D, dtype=F32), shape(1, 3, dtype=F32),
        shape(3, 1, FF, dtype=F32), shape(1, 12, dtype=F32), shape(12, 1, D, dtype=F32), shape(1, 3, dtype=F32),
    ]
    final = pl.pallas_call(
        unpack_kernel, out_shape=outs + grads, in_specs=whole(6), out_specs=whole(13)
    )(*computed)
    return tuple(
        jnp.swapaxes(item, 0, 1) if i >= 3 and item.ndim == 3 else item for i, item in enumerate(final)
    )


def solution(mesh):
    latents = P(("dp", "fsdp"), None, None)
    rows = P(None, ("dp", "fsdp"), None)
    entries = P(None, ("dp", "fsdp"))
    weights = (rows, entries) * 5
    return jax.shard_map(
        local,
        mesh=mesh,
        in_specs=(latents, P(("dp", "fsdp"), None), *weights, latents),
        out_specs=(latents, latents, P(("dp", "fsdp"), None), *weights),
        check_vma=False,
    )
```

time: 92.1 us -> 73.7 us (0.80)
  Pallas kernels: 84.1 us -> 72.7 us
  local copies, waits for them, and re-layouts: 6.75 us -> 0 us
    pallas_call x4 -> x2, Pallas kernels: 84.1 us -> 72.7 us  [the longest x1 70.7 us: local(): pl.pallas_call(block_kernel, out_shape=outs + [shape(16, 768, dtype=F32),...]
    unnamed x5 -> x0, local copies, waits for them, and re-layouts: 6.75 us -> none
where the time goes in v2:
time: 73.7 us; the launch traced here: 73.5 us
  Pallas kernels  72.7 us (99%)
  between operations  0.82 us (1%)
    pallas_call x1, Pallas kernels, local(): pl.pallas_call(block_kernel, out_shape=outs + [shape(16, 768, dtype=F32),...  70.7 us
    pallas_call x1, Pallas kernels, local(): pl.pallas_call(unpack_kernel, out_shape=outs + grads, in_specs=whole(6),...  2.03 us

profile of v2, /device:TPU:1, one launch (start us, length us, event | category | flops | bytes accessed | tf_op | source)
XLA Modules:
  0.0 73.5 jit_solution(16199302745940831515)
XLA Ops:
  0.6 70.7 %shard_map.228 = (bf16[1,256,384]{2,1,0:T(8,128)(2,1)}, f32[1,256,384]{2,1,0:T(8,128)}, f32[1,384]{1,0:T(1,128)}, f32[16,768]{1,0:T(8,128)}, f32[16,384]{1,0:T(8,128)}, /*index=5*/f32[8,2432]{1,0:T(8,128)}) custom-call(bf16[1,256,384]{2,1,0:T(8,128)(2,1)} %tokens.1, bf16[1,384]{1,0:T(2,128)(2,1)} %condition.1, bf16[1,3,2304]{2,1,0:T(4,128)(2,1)} %mod.1, ...), custom_call_target="tpu_custom_call" | custom-call | tf_op jit(solution)/shard_map/pallas_call | solution.py:626
  71.4 2.0 %shard_map.229 = (bf16[1,256,384]{2,1,0:T(8,128)(2,1)}, f32[1,256,384]{2,1,0:T(8,128)}, f32[1,384]{1,0:T(1,128)}, f32[3,1,2304]{2,1,0:T(1,128)}, f32[1,18]{1,0:T...) custom-call(bf16[1,256,384]{2,1,0:T(8,128)(2,1)} %get-tuple-element., ...), custom_call_target="tpu_custom_call" | custom-call | tf_op jit(solution)/shard_map/pallas_call | solution.py:652

commit v3 on v2

--- a/solution.py
+++ b/solution.py
@@ -18,7 +18,7 @@
 
 PARTS = 3
 ORDERS = ((0, 1, 2), (1, 2, 0), (2, 0, 1))
-BIASES = {"mod": (18, 0, 0), "attend": (6, 18, 0), "output": (3, 24, 6), "up": (12, 27, 9), "down": (3, 39, 21)}
+BIASES = {"mod": (18, 0), "attend": (6, 18), "output": (3, 24), "up": (12, 27), "down": (3, 39)}
 
 
 def dot(a, b, ca=1, cb=0):
@@ -36,6 +36,11 @@
 def device(at, core):
     x, y, z = at
     return (z * 16 + lax.rem(x, 2) * 8 + y * 2 + core, lax.div(x, 2))
+
+
+def owner_of(at, core):
+    x, y, z = at
+    return z * 32 + (x & 1) * 16 + y * 4 + core * 2 + (x >> 1)
 
 
 def moved(at, axis, by):
@@ -138,24 +143,25 @@
         return lax.rem(self.at[ORDERS[p][2]] + by, 4) * 16
 
     def across(self, p):
-        for by in (2, 1, 3, 0):
-            lo = self.chunk(p, by)
-            src = self.packed.at[p, pl.ds((1 - self.core) * 64 + lo, 16)]
-            self.start(0, p, by, src, self.chip.at[p, pl.ds(lo, 16)], None, 0)
+        self.start(0, p, 0, self.packed.at[p, pl.ds((1 - self.core) * 64, 64)], self.chip.at[p], None, 0)
 
     def third(self, p):
+        self.arrived(0, p, (0,))
         for by in (2, 1, 3, 0):
             lo = self.chunk(p, by)
             here = pl.ds(lo, 16)
-            self.arrived(0, p, (by,))
-            self.ours[p, here] = add(self.packed[p, pl.ds(self.core * 64 + lo, 16)], self.chip[p, here]).astype(BF16)
+            self.ours[p, here] = self.packed[p, pl.ds(self.core * 64 + lo, 16)] + self.chip[p, here]
             if by:
                 self.start(1, p, by, self.ours.at[p, here], self.ring.at[p, by - 1], ORDERS[p][2], by)
 
-    def second(self, p):
+    def second(self, p, more=None):
         self.arrived(1, p, (1, 3, 2))
         ring = self.ring
-        self.joined[p] = add(self.ours[p, pl.ds(self.chunk(p, 0), 16)], ring[p, 0], ring[p, 1], ring[p, 2]).astype(BF16)
+        wide = ring.shape[-1]
+        summed = add(self.ours[p, pl.ds(self.chunk(p, 0), 16)], ring[p, 0], ring[p, 1], ring[p, 2]).astype(BF16)
+        self.joined[p, :, :, 0:wide] = summed
+        if more is not None:
+            self.joined[p, :, :, wide:] = more
         b = ORDERS[p][1]
         for d in (2, 1, 3):
             src = self.joined.at[p, pl.ds(lax.rem(self.at[b] + d, 4) * 4, 4)]
@@ -238,9 +244,30 @@
 
 
 def bias_block(row, name):
-    mine, lane = bias_map(name, row.shape[1], BIASES[name][2])
+    mine, lane = bias_map(name, row.shape[1], BIASES[name][1])
     placed = jnp.where(mine, row, 0.0).astype(BF16)
     return dot(placed, jnp.where(lane, 1.0, 0.0).astype(BF16), 1, 1)
+
+
+def weighing(p, at, core, cact_all):
+    a, b, c = ORDERS[p]
+
+    def along(c_at, core_at, b_at, a_at):
+        spot = {c: c_at, b: b_at, a: a_at}
+        return owner_of((spot[0], spot[1], spot[2]), core_at)
+
+    latent = lax.broadcasted_iota(jnp.int32, (64, 128), 0) >> 3
+    here = along(latent >> 1, latent & 1, at[b], at[a])
+    pick = jnp.where(here == lax.broadcasted_iota(jnp.int32, (64, 128), 1), 1.0, 0.0).astype(BF16)
+    cacts = dot(pick, cact_all).astype(BF16)
+    n = lax.broadcasted_iota(jnp.int32, (256, D), 0)
+    row = n & 15
+    section = (row * 11) >> 5
+    feature = 3 * along(at[c], core, n >> 6, (n >> 4) & 3) + row - 3 * section
+    chosen = jnp.where((feature == lax.broadcasted_iota(jnp.int32, (256, D), 1)) & (row < 9), 1.0, 0.0).astype(BF16)
+    weights = dot(chosen, cacts, 1, 1)
+    row = lax.broadcasted_iota(jnp.int32, (256, 64), 0) & 15
+    return jnp.where((row * 11) >> 5 == (lax.broadcasted_iota(jnp.int32, (256, 64), 1) & 7), weights, 0.0).astype(BF16)
 
 
 def normalize(v):
@@ -262,7 +289,7 @@
 def block_kernel(
     tokens, condition, mod, b_mod, att, b_att, out, b_out, up, b_up, down, b_down, cotangent,
     result, token_grad, condition_grad, grad_ff, grad_att, grad_mod,
-    held1, held2, held3, w_mod, w_att, w_out, w_up, w_down, bias, cact_all,
+    held1, held2, pair_vectors, vectors, w_mod, w_att, w_out, w_up, w_down, bias, cact_all,
     d_att, d_out, d_up, d_down, probs_ref,
     packed, chip, ours, ring, joined, row, near, line, ends,
     packed_a, chip_a, ours_a, ring_a, joined_a, row_a, near_a, line_a, ends_a,
@@ -270,9 +297,8 @@
 ):
     at, core = place()
     announce(at, core)
-    first, second, third = [
-        Gather(at, core, held, sems.at[i, 0], sems.at[i, 1]) for i, held in enumerate((held1, held2, held3))
-    ]
+    first, second = [Gather(at, core, held, sems.at[i, 0], sems.at[i, 1]) for i, held in enumerate((held1, held2))]
+    trade = Moves(at, core, sems.at[2, 0], sems.at[2, 1])
     back = Reduce(at, core, packed, chip, ours, ring, joined, row, near, line, ends, sems.at[3, 0], sems.at[3, 1])
     last = Reduce(
         at, core, packed_a, chip_a, ours_a, ring_a, joined_a, row_a, near_a, line_a, ends_a, sems.at[4, 0], sems.at[4, 1]
@@ -407,6 +433,7 @@
         high = dot(right, jnp.concatenate([blocks[1][:, 128:], blocks[2]], axis=1))
         w_down[192 * group : 192 * group + 192, :] = (low + high).astype(BF16)
 
+    weights = [weighing(p, at, core, cact_all[...]) for p in range(PARTS)]
     b_upper = bias_row(raw_bias, "up", FF)
     dfeed = (gate2 * g).astype(BF16)
     feed = jnp.zeros((S, D), F32)
@@ -480,13 +507,24 @@
         dq.append((jnp.concatenate(dq_t, axis=0).T * FACTOR).astype(BF16))
         dk.append((jnp.where(halves[0], dk_h[0], dk_h[1]) * FACTOR).astype(BF16))
         dv.append(jnp.where(halves[0], dv_h[0], dv_h[1]).astype(BF16))
-        back.third(i)
+        if i == 1:
+            back.third(0)
+            back.third(1)
+    back.third(2)
     dtriple = jnp.concatenate(dq + dk + dv, axis=1)
+    dhidden1 = dot(dtriple, w_att[...], 1, 1)
+    dscale1, dshift1 = total(dhidden1 * n1), total(dhidden1)
+    dmod = jnp.concatenate([dshift1, dscale1, dgate1, dshift2, dscale2, dgate2], axis=1)
+    sections = jnp.concatenate([dmod[:, 768 * i : 768 * i + 768] for i in range(3)] + [jnp.zeros((5, 768), F32)], axis=0)
+    for p in range(PARTS):
+        pair_vectors[core, p] = sections[:, 256 * p : 256 * p + 256]
+    trade.start(0, 0, 0, pair_vectors.at[core], pair_vectors.at[core], None, 0)
     d_att[...] = dot(hidden1.T, dtriple).astype(BF16)
     sums = total(dtriple.astype(F32))
     db_att = jnp.concatenate([sums[:, :D], sums[:, 2 * D :]], axis=1)
     d_bias = (
-        bias_block(db_att, "attend")
+        bias_block(dmod, "mod")
+        + bias_block(db_att, "attend")
         + bias_block(db_out, "output")
         + bias_block(jnp.concatenate(db_up, axis=1), "up")
         + bias_block(db_down, "down")
@@ -503,22 +541,17 @@
     for p in range(PARTS):
         last.across(p)
 
-    dhidden1 = dot(dtriple, w_att[...], 1, 1)
-    dscale1, dshift1 = total(dhidden1 * n1), total(dhidden1)
-    dmods = [dshift1, dscale1, dgate1, dshift2, dscale2, dgate2]
-    vectors = jnp.concatenate(dmods + [jnp.zeros((2, D), F32)], axis=0)
-    for p in range(PARTS):
-        held3[p, third.own(p)] = vectors[:, 128 * p : 128 * p + 128]
-        third.first(p)
+    trade.arrived(0, 0, (0,))
+    for p in range(PARTS):
+        c = ORDERS[p][2]
+        for d in (1, 3, 2):
+            trade.start(1, p, d, pair_vectors.at[:, p], vectors.at[p, at[c]], c, d)
+        vectors[p, at[c]] = pair_vectors[:, p]
     for p in range(PARTS):
         last.third(p)
     for p in range(PARTS):
         back.second(p)
     token_grad[0] = gmid + denormalize(dhidden1 * (1.0 + scale1), n1, inverse1)
-    for p in range(PARTS):
-        third.second(p)
-
-    dmod = jnp.concatenate(dmods, axis=1)
     dcact = jnp.zeros((D, 128), F32)
     for t in range(18):
         here = slice(128 * t, 128 * t + 128)
@@ -526,54 +559,21 @@
     condition_grad[...] = total(dcact.T) * (sigmoid * (1.0 + cond * (1.0 - sigmoid)))
 
     for p in range(PARTS):
-        last.second(p)
+        trade.arrived(1, p, (1, 3, 2))
+    d_mod = [dot(weights[p], vectors[p].reshape(64, 256).astype(BF16)).astype(BF16) for p in range(PARTS)]
+    for p in range(PARTS):
+        last.second(p, d_mod[p].reshape(16, 16, 256))
     for p in range(PARTS):
         back.first(p)
     for p in range(PARTS):
-        third.third(p)
-
-    index = 2 * lax.axis_index("dp") + lax.axis_index("fsdp")
-    feature = lax.broadcasted_iota(jnp.int32, (8, D), 1)
-    r = lax.broadcasted_iota(jnp.int32, (8, D), 0)
-    pick = jnp.where((feature == 3 * index + r) & (r < 3), 1.0, 0.0).astype(BF16)
-    columns = dot(pick, cact_all[...], 1, 1).astype(BF16)
-    natural = lax.broadcasted_iota(jnp.int32, (128, 1024), 0)
-    j = lax.broadcasted_iota(jnp.int32, (128, 1024), 1) >> 3
-    stacked = lax.broadcasted_iota(jnp.int32, (64, 1024), 0)
-    inner = lax.broadcasted_iota(jnp.int32, (64, 1024), 1) & 7
-    weighing = []
-    for p in range(PARTS):
-        a, b, c = ORDERS[p]
-        coordinate = {c: (j >> 4) & 3, b: (j >> 2) & 3, a: j & 3}
-        xj, yj, zj = coordinate[0], coordinate[1], coordinate[2]
-        source = zj * 32 + (xj & 1) * 16 + yj * 4 + (j >> 6) * 2 + (xj >> 1)
-        expanded = dot(columns, jnp.where(source == natural, 1.0, 0.0).astype(BF16))
-        tiled = jnp.concatenate([expanded] * 8, axis=0)
-        tiled = jnp.where((stacked & 7) == 3, 1.0, tiled)
-        weighing.append(jnp.where((stacked >> 3) == inner, tiled, 0.0).astype(BF16))
-
-    for p in range(PARTS):
         last.first(p)
     for p in range(PARTS):
         grad_ff[:, 256 * p : 256 * p + 256] = back.total(p)
-    for d in (1, 3, 2):
-        for p in range(PARTS):
-            third.across(p, d)
-    for p in range(PARTS):
-        grad_att[:, 128 * p : 128 * p + 128] = last.total(p)
-    weighed = []
-    for p in range(PARTS):
-        third.complete(p)
-        weighed.append(dot(weighing[p], held3[p].reshape(1024, 128).astype(BF16)))
-    grads = jnp.concatenate(
-        [weighed[p][8 * i : 8 * i + 8] for i in range(6) for p in range(PARTS)], axis=1
-    )
-    n = lax.broadcasted_iota(jnp.int32, (6 * D, 128), 0)
-    k = lax.broadcasted_iota(jnp.int32, (6 * D, 128), 1)
-    mine = jnp.where((n == 18 * index + k) & (k < 18), 1.0, 0.0).astype(BF16)
-    grad_mod[:, 0 : 6 * D] = grads
-    grad_mod[:, 6 * D :] = dot(grads.astype(BF16), mine)
-    for moves in (first, second, third, back, last):
+    for p in range(PARTS):
+        summed = last.total(p)
+        grad_att[:, 128 * p : 128 * p + 128] = summed[:, 0:128]
+        grad_mod[:, 256 * p : 256 * p + 256] = summed[:, 128:384]
+    for moves in (first, second, trade, back, last):
         moves.sent()
 
 
@@ -584,16 +584,15 @@
     result[...] = result_in[...]
     token_grad[...] = token_in[...]
     condition_grad[...] = condition_in[...]
-    mod[:, 0, :] = modulation[0:3, 0 : 6 * D]
-    b_mod[...] = modulation[3:4, 6 * D : 6 * D + 18]
     for i in range(3):
+        mod[:, 0, 768 * i : 768 * i + 768] = modulation[3 * i : 3 * i + 3, :]
         att[:, 0, D * i : D * i + D] = attend[3 * i : 3 * i + 3, :]
     for i in range(2):
         up[:, 0, 768 * i : 768 * i + 768] = ff[3 * i : 3 * i + 3, :]
         down[6 * i : 6 * i + 6, 0, :] = ff[6:12, D * i : D * i + D]
     out[:, 0, :] = ff[12:15, 0:D]
-    for ref, name in ((b_att, "attend"), (b_out, "output"), (b_up, "up"), (b_down, "down")):
-        size, _, lane = BIASES[name]
+    for ref, name in ((b_mod, "mod"), (b_att, "attend"), (b_out, "output"), (b_up, "up"), (b_down, "down")):
+        size, lane = BIASES[name]
         ref[...] = attend[9:10, lane : lane + size]
 
 
@@ -605,17 +604,17 @@
     return jax.ShapeDtypeStruct(dims, dtype)
 
 
-def reduce_scratch(wide):
+def reduce_scratch(wide, wider):
     return [
         pltpu.VMEM((PARTS, 128, 16, wide), BF16),
         pltpu.VMEM((PARTS, 64, 16, wide), BF16),
         pltpu.VMEM((PARTS, 64, 16, wide), BF16),
         pltpu.VMEM((PARTS, 3, 16, 16, wide), BF16),
-        pltpu.VMEM((PARTS, 16, 16, wide), BF16),
-        pltpu.VMEM((PARTS, 3, 4, 16, wide), BF16),
-        pltpu.VMEM((PARTS, 4, 16, wide), F32),
-        pltpu.VMEM((PARTS, 4, 16, wide), BF16),
-        pltpu.VMEM((PARTS, 3, 16, wide), BF16),
+        pltpu.VMEM((PARTS, 16, 16, wider), BF16),
+        pltpu.VMEM((PARTS, 3, 4, 16, wider), BF16),
+        pltpu.VMEM((PARTS, 4, 16, wider), F32),
+        pltpu.VMEM((PARTS, 4, 16, wider), BF16),
+        pltpu.VMEM((PARTS, 3, 16, wider), BF16),
     ]
 
 
@@ -625,19 +624,20 @@
     ]
     computed = pl.pallas_call(
         block_kernel,
-        out_shape=outs + [shape(16, 768, dtype=F32), shape(16, D, dtype=F32), shape(8, 6 * D + 128, dtype=F32)],
+        out_shape=outs + [shape(16, 768, dtype=F32), shape(16, D, dtype=F32), shape(16, 768, dtype=F32)],
         in_specs=whole(13),
         out_specs=whole(6),
         scratch_shapes=[
             pltpu.VMEM((PARTS, 128, 16, 256), BF16),
             pltpu.VMEM((PARTS, 128, 16, 256), BF16),
-            pltpu.VMEM((PARTS, 128, 8, 128), F32),
+            pltpu.VMEM((2, PARTS, 8, 256), F32),
+            pltpu.VMEM((PARTS, 4, 2, 8, 256), F32),
             pltpu.VMEM((D, 6 * D), BF16), pltpu.VMEM((D, 3 * D), BF16), pltpu.VMEM((D, D), BF16),
             pltpu.VMEM((D, FF), BF16), pltpu.VMEM((FF, D), BF16), pltpu.VMEM((128, 128), BF16), pltpu.VMEM((128, D), BF16),
             pltpu.VMEM((D, 3 * D), BF16), pltpu.VMEM((D, D), BF16),
             pltpu.VMEM((D, FF), BF16), pltpu.VMEM((FF, D), BF16), pltpu.VMEM((6, S, S), F32),
-            *reduce_scratch(256),
-            *reduce_scratch(128),
+            *reduce_scratch(256, 256),
+            *reduce_scratch(128, 384),
             pltpu.SemaphoreType.DMA((5, 2, 4, PARTS, 4)),
         ],
         compiler_params=pltpu.CompilerParams(

time: 73.7 us -> 70.9 us (0.962)
  Pallas kernels: 72.7 us -> 69.7 us
    pallas_call x1, Pallas kernels: 70.7 us -> 67.7 us  [local(): pl.pallas_call(block_kernel, out_shape=outs + [shape(16, 768, dtype=F32),...]
where the time goes in v3:
time: 70.9 us; the launch traced here: 70.5 us
  Pallas kernels  69.7 us (98%)
  between operations  0.82 us (1%)
    pallas_call x1, Pallas kernels, local(): pl.pallas_call(block_kernel, out_shape=outs + [shape(16, 768, dtype=F32),...  67.7 us
    pallas_call x1, Pallas kernels, local(): pl.pallas_call(unpack_kernel, out_shape=outs + grads, in_specs=whole(6),...  1.97 us

profile of v3, /device:TPU:1, one launch (start us, length us, event | category | flops | bytes accessed | tf_op | source)
XLA Modules:
  0.0 70.5 jit_solution(6533594305921084683)
XLA Ops:
  0.6 67.7 %shard_map.228 = (bf16[1,256,384]{2,1,0:T(8,128)(2,1)}, f32[1,256,384]{2,1,0:T(8,128)}, f32[1,384]{1,0:T(1,128)}, f32[16,768]{1,0:T(8,128)}, f32[16,384]{1,0:T(8,128)}, /*index=5*/f32[16,768]{1,0:T(8,128)}) custom-call(bf16[1,256,384]{2,1,0:T(8,128)(2,1)} %tokens.1, bf16[1,384]{1,0:T(2,128)(2,1)} %condition.1, bf16[1,3,2304]{2,1,0:T(4,128)(2,1)} %mod.1, ...), custom_call_target="tpu_custom_call" | custom-call | tf_op jit(solution)/shard_map/pallas_call | solution.py:625
  68.4 2.0 %shard_map.229 = (bf16[1,256,384]{2,1,0:T(8,128)(2,1)}, f32[1,256,384]{2,1,0:T(8,128)}, f32[1,384]{1,0:T(1,128)}, f32[3,1,2304]{2,1,0:T(1,128)}, f32[1,18]{1,0:T...) custom-call(bf16[1,256,384]{2,1,0:T(8,128)(2,1)} %get-tuple-element., ...), custom_call_target="tpu_custom_call" | custom-call | tf_op jit(solution)/shard_map/pallas_call | solution.py:652

commit v4 on v3

--- a/solution.py
+++ b/solution.py
@@ -199,24 +199,19 @@
     return jnp.where(row == 15, 240 + member, threes(member, row))
 
 
-def place_up(member, row):
-    return jnp.where(row < 6, threes(member, row), -1)
-
-
-def place_left(member, row):
-    return jnp.where((row >= 6) & (row < 12), member * 12 + row - 6, -1)
-
-
-def place_right(member, row):
-    return jnp.where((row >= 6) & (row < 12), member * 12 + row, -1)
-
-
-def place_back(member, row):
-    return jnp.where(row < 6, threes(member, row), jnp.where((row >= 12) & (row < 15), threes(member, row) - 96, -1))
+def shuffle(transposed):
+    n = lax.broadcasted_iota(jnp.int32, (D, D), 0 if transposed else 1)
+    o = lax.broadcasted_iota(jnp.int32, (D, D), 1 if transposed else 0)
+    member, row = (n >> 3) & 15, n & 7
+    item = 4 * (n >> 7) + (row & 3)
+    quarter = (item * 11) >> 5
+    up = 48 * quarter + 3 * member + item - 3 * quarter
+    return jnp.where(jnp.where(row < 4, up, 192 + 12 * member + item) == o, 1.0, 0.0).astype(BF16)
 
 
 def place_attend(member, row):
-    return jnp.where(row < 9, threes(member, row), jnp.where(row == 9, 144 + member, -1))
+    small = jnp.where(row == 9, 144 + member, 160 + member * 3 + row - 10)
+    return jnp.where(row < 9, threes(member, row), jnp.where(row < 13, small, -1))
 
 
 def members(part, group):
@@ -229,24 +224,22 @@
     ]
 
 
-def bias_map(name, count, lane):
-    size = BIASES[name][0]
+def bias_map(name, count):
+    size, lane = BIASES[name]
     n = lax.broadcasted_iota(jnp.int32, (128, count), 1)
     owner = (n * -(-65536 // size)) >> 16
     k = lax.broadcasted_iota(jnp.int32, (128, count), 0)
-    return owner == k, (n - owner * size + lane) == k
-
-
-def bias_row(bias, name, count):
-    mine, lane = bias_map(name, count, BIASES[name][1])
-    picked = dot(bias, jnp.where(lane, 1.0, 0.0).astype(BF16))
-    return jnp.sum(jnp.where(mine, picked, 0.0), axis=0, keepdims=True)
-
-
-def bias_block(row, name):
-    mine, lane = bias_map(name, row.shape[1], BIASES[name][1])
-    placed = jnp.where(mine, row, 0.0).astype(BF16)
-    return dot(placed, jnp.where(lane, 1.0, 0.0).astype(BF16), 1, 1)
+    return [jnp.where(hit, 1.0, 0.0).astype(BF16) for hit in (owner == k, n - owner * size + lane == k)]
+
+
+def bias_row(bias, maps):
+    mine, lane = maps
+    return jnp.sum(dot(bias, lane) * mine.astype(F32), axis=0, keepdims=True)
+
+
+def bias_block(row, maps):
+    mine, lane = maps
+    return dot((mine.astype(F32) * row).astype(BF16), lane, 1, 1)
 
 
 def weighing(p, at, core, cact_all):
@@ -320,14 +313,12 @@
          jnp.concatenate([load(att, 768, 1152), load(out, 0, 384)], axis=1), bias_line],
         axis=0,
     ).astype(BF16)
+    quarters = jnp.concatenate([load(up, D * i, D * i + D) for i in range(4)], axis=0)
     tall = down[0].astype(F32)
-    mine2 = jnp.concatenate(
-        [load(up, 0, 768), load(up, 768, 1536), jnp.concatenate([tall[0:6], tall[6:12]], axis=1), jnp.zeros((4, 768), F32)],
-        axis=0,
-    ).astype(BF16)
     for p in range(PARTS):
         held1[p, first.own(p)] = mine[:, 256 * p : 256 * p + 256]
-        held2[p, second.own(p)] = mine2[:, 256 * p : 256 * p + 256]
+        items = slice(4 * p, 4 * p + 4)
+        held2[p, second.own(p)] = jnp.concatenate([quarters[items], tall[items]], axis=0).astype(BF16)
 
     pl.semaphore_wait(pltpu.get_barrier_semaphore(), 10)
     for p in range(PARTS):
@@ -339,11 +330,14 @@
     g = cotangent[0].astype(F32)
     cact_column = jnp.broadcast_to(cact, (128, D)).T
     n1, inverse1 = normalize(x)
+    maps = {name: bias_map(name, 128 * BIASES[name][0]) for name in BIASES}
+    first_rows = spread(place_first, 256, False)
 
     for p in range(PARTS):
         first.second(p)
     for p in range(PARTS):
         second.second(p)
+    shuffled, unshuffled, attend_rows = shuffle(False), shuffle(True), spread(place_attend, 208, True)
     for p in range(PARTS):
         first.third(p)
     for p in range(PARTS):
@@ -352,14 +346,13 @@
         for p in range(PARTS):
             first.across(p, d)
 
-    rows = spread(place_first, 256, False)
     for p in range(PARTS):
         first.complete(p)
         lo = 256 * p
         for group in range(8):
             here = slice(48 * group, 48 * group + 48)
             few = slice(16 * group, 16 * group + 16)
-            laid = dot(rows, jnp.concatenate([held1[p, s] for s in members(p, group)], axis=0)).astype(BF16)
+            laid = dot(first_rows, jnp.concatenate([held1[p, s] for s in members(p, group)], axis=0)).astype(BF16)
             for i in range(3):
                 w_mod[here, 768 * i + lo : 768 * i + lo + 256] = laid[48 * i : 48 * i + 48]
             w_att[here, lo : lo + 256] = laid[144:192]
@@ -378,12 +371,12 @@
     modulation = jnp.concatenate(
         [total(w_mod[:, 128 * t : 128 * t + 128].astype(F32) * cact_column) for t in range(18)],
         axis=1,
-    ) + bias_row(raw_bias, "mod", 6 * D)
+    ) + bias_row(raw_bias, maps["mod"])
     shift1, scale1, gate1, shift2, scale2, gate2 = [
         modulation[:, D * i : D * i + D] for i in range(6)
     ]
     hidden1 = (n1 * (1.0 + scale1) + shift1).astype(BF16)
-    b_attend = bias_row(raw_bias, "attend", 2 * D)
+    b_attend = bias_row(raw_bias, maps["attend"])
     b_full = jnp.concatenate([b_attend[:, :D], jnp.zeros((1, D), F32), b_attend[:, D:]], axis=1)
     triple = (dot(hidden1, w_att[...]) + b_full).astype(BF16)
 
@@ -391,6 +384,9 @@
         lo = D * which + 128 * i
         return triple[:, lo : lo + 128]
 
+    weights = [weighing(p, at, core, cact_all[...]) for p in range(PARTS)]
+    b_output, b_upper, b_lower = [bias_row(raw_bias, maps[name]) for name in ("output", "up", "down")]
+    dfeed = (gate2 * g).astype(BF16)
     for d in (1, 3, 2):
         for p in range(PARTS):
             second.across(p, d)
@@ -413,29 +409,23 @@
             mixed_t.append(dot(v_t[64 * h : 64 * h + 64], probs.astype(BF16)))
         mixed_pairs.append(jnp.concatenate(mixed_t, axis=0).T.astype(BF16))
     mixed = jnp.concatenate(mixed_pairs, axis=1)
-    branch = dot(mixed, w_out[...]) + bias_row(raw_bias, "output", D)
+    branch = dot(mixed, w_out[...]) + b_output
     middle = x + gate1 * branch
     n2, inverse2 = normalize(middle)
     hidden2 = (n2 * (1.0 + scale2) + shift2).astype(BF16)
 
-    rows = spread(place_up, 96, False)
-    left, right = spread(place_left, 192, False), spread(place_right, 192, False)
     for p in range(PARTS):
         second.complete(p)
     for group in range(8):
         here = slice(48 * group, 48 * group + 48)
-        blocks = [jnp.concatenate([held2[p, s] for s in members(p, group)], axis=0) for p in range(PARTS)]
-        for p in range(PARTS):
-            laid = dot(rows, blocks[p]).astype(BF16)
-            w_up[here, 256 * p : 256 * p + 256] = laid[0:48]
-            w_up[here, 768 + 256 * p : 1024 + 256 * p] = laid[48:96]
-        low = dot(left, jnp.concatenate([blocks[0], blocks[1][:, :128]], axis=1))
-        high = dot(right, jnp.concatenate([blocks[1][:, 128:], blocks[2]], axis=1))
-        w_down[192 * group : 192 * group + 192, :] = (low + high).astype(BF16)
-
-    weights = [weighing(p, at, core, cact_all[...]) for p in range(PARTS)]
-    b_upper = bias_row(raw_bias, "up", FF)
-    dfeed = (gate2 * g).astype(BF16)
+        blocks = jnp.concatenate(
+            [held2[p, s].astype(F32) for p in range(PARTS) for s in members(p, group)], axis=0
+        ).astype(BF16)
+        laid = dot(shuffled, blocks).astype(BF16)
+        for i in range(4):
+            w_up[here, D * i : D * i + D] = laid[48 * i : 48 * i + 48]
+        w_down[192 * group : 192 * group + 192, :] = laid[192:384]
+
     feed = jnp.zeros((S, D), F32)
     dhidden2 = jnp.zeros((S, D), F32)
     db_up = []
@@ -456,7 +446,7 @@
         d_up[:, lo : lo + D] = dot(hidden2_t, dupper).astype(BF16)
         db_up.append(total(dupper.astype(F32)))
         dhidden2 = dhidden2 + dot(dupper, w_up[:, lo : lo + D], 1, 1)
-    feed = feed + bias_row(raw_bias, "down", D)
+    feed = feed + b_lower
     result[0] = (middle + gate2 * feed).astype(BF16)
     dgate2 = total(g * feed)
     db_down = total(dfeed.astype(F32))
@@ -467,27 +457,16 @@
     d_out[...] = dot(mixed.T, dbranch).astype(BF16)
     db_out = total(dbranch.astype(F32))
 
-    rows = spread(place_back, 144, True)
-    left, right = spread(place_left, 192, True), spread(place_right, 192, True)
-    for p in range(PARTS):
-        for group in range(8):
-            here = slice(48 * group, 48 * group + 48)
-            tall = slice(192 * group, 192 * group + 192)
-            if p == 0:
-                extra = d_out[here, 0:256]
-                stretched = dot(left, d_down[tall, 0:256])
-            elif p == 1:
-                extra = jnp.concatenate([d_out[here, 256:384], jnp.zeros((48, 128), BF16)], axis=1)
-                stretched = jnp.concatenate([dot(left, d_down[tall, 256:384]), dot(right, d_down[tall, 0:128])], axis=1)
-            else:
-                extra = jnp.zeros((48, 256), BF16)
-                stretched = dot(right, d_down[tall, 128:384])
-            flat = jnp.concatenate(
-                [d_up[here, 256 * p : 256 * p + 256], d_up[here, 768 + 256 * p : 1024 + 256 * p], extra], axis=0
-            )
-            laid = (dot(rows, flat) + stretched).astype(BF16)
+    for group in range(8):
+        here = slice(48 * group, 48 * group + 48)
+        flat = jnp.concatenate(
+            [d_up[here, D * i : D * i + D] for i in range(4)] + [d_down[192 * group : 192 * group + 192, :]], axis=0
+        )
+        laid = dot(unshuffled, flat)
+        for p in range(PARTS):
             for m, s in enumerate(members(p, group)):
-                packed[p, s] = laid[16 * m : 16 * m + 16]
+                packed[p, s] = laid[128 * p + 8 * m : 128 * p + 8 * m + 8].astype(BF16)
+    for p in range(PARTS):
         back.across(p)
 
     dmixed = dot(dbranch, w_out[...], 1, 1).astype(BF16)
@@ -507,10 +486,8 @@
         dq.append((jnp.concatenate(dq_t, axis=0).T * FACTOR).astype(BF16))
         dk.append((jnp.where(halves[0], dk_h[0], dk_h[1]) * FACTOR).astype(BF16))
         dv.append(jnp.where(halves[0], dv_h[0], dv_h[1]).astype(BF16))
-        if i == 1:
-            back.third(0)
-            back.third(1)
-    back.third(2)
+    for p in range(PARTS):
+        back.third(p)
     dtriple = jnp.concatenate(dq + dk + dv, axis=1)
     dhidden1 = dot(dtriple, w_att[...], 1, 1)
     dscale1, dshift1 = total(dhidden1 * n1), total(dhidden1)
@@ -523,18 +500,17 @@
     sums = total(dtriple.astype(F32))
     db_att = jnp.concatenate([sums[:, :D], sums[:, 2 * D :]], axis=1)
     d_bias = (
-        bias_block(dmod, "mod")
-        + bias_block(db_att, "attend")
-        + bias_block(db_out, "output")
-        + bias_block(jnp.concatenate(db_up, axis=1), "up")
-        + bias_block(db_down, "down")
+        bias_block(dmod, maps["mod"])
+        + bias_block(db_att, maps["attend"])
+        + bias_block(db_out, maps["output"])
+        + bias_block(jnp.concatenate(db_up, axis=1), maps["up"])
+        + bias_block(db_down, maps["down"])
     ).astype(BF16)
-    rows = spread(place_attend, 160, True)
     for group in range(8):
         here = slice(48 * group, 48 * group + 48)
         biases = jnp.concatenate([d_bias[16 * group : 16 * group + 16], jnp.zeros((16, 256), BF16)], axis=1)
-        flat = jnp.concatenate([d_att[here, 0:384], d_att[here, 384:768], d_att[here, 768:1152], biases], axis=0)
-        laid = dot(rows, flat).astype(BF16)
+        flat = jnp.concatenate([d_att[here, 0:384], d_att[here, 384:768], d_att[here, 768:1152], biases, d_out[here, :]], axis=0)
+        laid = dot(attend_rows, flat).astype(BF16)
         for p in range(PARTS):
             for m, s in enumerate(members(p, group)):
                 packed_a[p, s] = laid[16 * m : 16 * m + 16, 128 * p : 128 * p + 128]
@@ -568,7 +544,7 @@
     for p in range(PARTS):
         last.first(p)
     for p in range(PARTS):
-        grad_ff[:, 256 * p : 256 * p + 256] = back.total(p)
+        grad_ff[8 * p : 8 * p + 8, :] = back.total(p)
     for p in range(PARTS):
         summed = last.total(p)
         grad_att[:, 128 * p : 128 * p + 128] = summed[:, 0:128]
@@ -587,10 +563,11 @@
     for i in range(3):
         mod[:, 0, 768 * i : 768 * i + 768] = modulation[3 * i : 3 * i + 3, :]
         att[:, 0, D * i : D * i + D] = attend[3 * i : 3 * i + 3, :]
-    for i in range(2):
-        up[:, 0, 768 * i : 768 * i + 768] = ff[3 * i : 3 * i + 3, :]
-        down[6 * i : 6 * i + 6, 0, :] = ff[6:12, D * i : D * i + D]
-    out[:, 0, :] = ff[12:15, 0:D]
+    for i in range(12):
+        lo = 8 * (i // 4) + i % 4
+        up[i % 3, :, D * (i // 3) : D * (i // 3) + D] = ff[lo : lo + 1, :]
+        down[i] = ff[lo + 4 : lo + 5, :]
+    out[:, 0, :] = attend[10:13, :]
     for ref, name in ((b_mod, "mod"), (b_att, "attend"), (b_out, "output"), (b_up, "up"), (b_down, "down")):
         size, lane = BIASES[name]
         ref[...] = attend[9:10, lane : lane + size]
@@ -604,17 +581,17 @@
     return jax.ShapeDtypeStruct(dims, dtype)
 
 
-def reduce_scratch(wide, wider):
+def reduce_scratch(tall, wide, wider):
     return [
-        pltpu.VMEM((PARTS, 128, 16, wide), BF16),
-        pltpu.VMEM((PARTS, 64, 16, wide), BF16),
-        pltpu.VMEM((PARTS, 64, 16, wide), BF16),
-        pltpu.VMEM((PARTS, 3, 16, 16, wide), BF16),
-        pltpu.VMEM((PARTS, 16, 16, wider), BF16),
-        pltpu.VMEM((PARTS, 3, 4, 16, wider), BF16),
-        pltpu.VMEM((PARTS, 4, 16, wider), F32),
-        pltpu.VMEM((PARTS, 4, 16, wider), BF16),
-        pltpu.VMEM((PARTS, 3, 16, wider), BF16),
+        pltpu.VMEM((PARTS, 128, tall, wide), BF16),
+        pltpu.VMEM((PARTS, 64, tall, wide), BF16),
+        pltpu.VMEM((PARTS, 64, tall, wide), BF16),
+        pltpu.VMEM((PARTS, 3, 16, tall, wide), BF16),
+        pltpu.VMEM((PARTS, 16, tall, wider), BF16),
+        pltpu.VMEM((PARTS, 3, 4, tall, wider), BF16),
+        pltpu.VMEM((PARTS, 4, tall, wider), F32),
+        pltpu.VMEM((PARTS, 4, tall, wider), BF16),
+        pltpu.VMEM((PARTS, 3, tall, wider), BF16),
     ]
 
 
@@ -624,20 +601,20 @@
     ]
     computed = pl.pallas_call(
         block_kernel,
-        out_shape=outs + [shape(16, 768, dtype=F32), shape(16, D, dtype=F32), shape(16, 768, dtype=F32)],
+        out_shape=outs + [shape(24, D, dtype=F32), shape(16, D, dtype=F32), shape(16, 768, dtype=F32)],
         in_specs=whole(13),
         out_specs=whole(6),
         scratch_shapes=[
             pltpu.VMEM((PARTS, 128, 16, 256), BF16),
-            pltpu.VMEM((PARTS, 128, 16, 256), BF16),
+            pltpu.VMEM((PARTS, 128, 8, D), BF16),
             pltpu.VMEM((2, PARTS, 8, 256), F32),
             pltpu.VMEM((PARTS, 4, 2, 8, 256), F32),
             pltpu.VMEM((D, 6 * D), BF16), pltpu.VMEM((D, 3 * D), BF16), pltpu.VMEM((D, D), BF16),
             pltpu.VMEM((D, FF), BF16), pltpu.VMEM((FF, D), BF16), pltpu.VMEM((128, 128), BF16), pltpu.VMEM((128, D), BF16),
             pltpu.VMEM((D, 3 * D), BF16), pltpu.VMEM((D, D), BF16),
             pltpu.VMEM((D, FF), BF16), pltpu.VMEM((FF, D), BF16), pltpu.VMEM((6, S, S), F32),
-            *reduce_scratch(256, 256),
-            *reduce_scratch(128, 384),
+            *reduce_scratch(8, D, D),
+            *reduce_scratch(16, 128, D),
             pltpu.SemaphoreType.DMA((5, 2, 4, PARTS, 4)),
         ],
         compiler_params=pltpu.CompilerParams(

time: 70.9 us -> 68.3 us (0.963)
  Pallas kernels: 69.7 us -> 66.5 us
    pallas_call x1, Pallas kernels: 67.7 us -> 64.5 us  [local(): pl.pallas_call(block_kernel, out_shape=outs + [shape(24, D, dtype=F32), s...]
where the time goes in v4:
time: 68.3 us; the launch traced here: 67.3 us
  Pallas kernels  66.5 us (97%)
  between operations  0.82 us (1%)
    pallas_call x1, Pallas kernels, local(): pl.pallas_call(block_kernel, out_shape=outs + [shape(24, D, dtype=F32), s...  64.5 us
    pallas_call x1, Pallas kernels, local(): pl.pallas_call(unpack_kernel, out_shape=outs + grads, in_specs=whole(6),...  1.97 us

profile of v4, /device:TPU:1, one launch (start us, length us, event | category | flops | bytes accessed | tf_op | source)
XLA Modules:
  0.0 67.3 jit_solution(16682394286319867088)
XLA Ops:
  0.6 64.5 %shard_map.228 = (bf16[1,256,384]{2,1,0:T(8,128)(2,1)}, f32[1,256,384]{2,1,0:T(8,128)}, f32[1,384]{1,0:T(1,128)}, f32[24,384]{1,0:T(8,128)}, f32[16,384]{1,0:T(8,128)}, /*index=5*/f32[16,768]{1,0:T(8,128)}) custom-call(bf16[1,256,384]{2,1,0:T(8,128)(2,1)} %tokens.1, bf16[1,384]{1,0:T(2,128)(2,1)} %condition.1, bf16[1,3,2304]{2,1,0:T(4,128)(2,1)} %mod.1, ...), custom_call_target="tpu_custom_call" | custom-call | tf_op jit(solution)/shard_map/pallas_call | solution.py:602
  65.2 2.0 %shard_map.229 = (bf16[1,256,384]{2,1,0:T(8,128)(2,1)}, f32[1,256,384]{2,1,0:T(8,128)}, f32[1,384]{1,0:T(1,128)}, f32[3,1,2304]{2,1,0:T(1,128)}, f32[1,18]{1,0:T...) custom-call(bf16[1,256,384]{2,1,0:T(8,128)(2,1)} %get-tuple-element., ...), custom_call_target="tpu_custom_call" | custom-call | tf_op jit(solution)/shard_map/pallas_call | solution.py:629

commit v5 on v4

--- a/solution.py
+++ b/solution.py
@@ -430,9 +430,9 @@
     dhidden2 = jnp.zeros((S, D), F32)
     db_up = []
     hidden2_t = hidden2.T
-    for c in range(4):
-        lo = D * c
-        upper = dot(hidden2, w_up[:, lo : lo + D]) + b_upper[:, lo : lo + D]
+    for c in range(2):
+        lo = 768 * c
+        upper = dot(hidden2, w_up[:, lo : lo + 768]) + b_upper[:, lo : lo + 768]
         square = upper * upper
         t = jnp.tanh(0.7978845608028654 * (upper + 0.044715 * (upper * square)))
         half = 0.5 * (1.0 + t)
@@ -440,12 +440,12 @@
         slope = half + (0.5 * upper) * (1.0 - t * t) * (
             0.7978845608028654 * (1.0 + 0.134145 * square)
         )
-        feed = feed + dot(activated, w_down[lo : lo + D, :])
-        dupper = (dot(dfeed, w_down[lo : lo + D, :], 1, 1) * slope).astype(BF16)
-        d_down[lo : lo + D, :] = dot(activated.T, dfeed).astype(BF16)
-        d_up[:, lo : lo + D] = dot(hidden2_t, dupper).astype(BF16)
+        feed = feed + dot(activated, w_down[lo : lo + 768, :])
+        dupper = (dot(dfeed, w_down[lo : lo + 768, :], 1, 1) * slope).astype(BF16)
+        d_down[lo : lo + 768, :] = dot(activated.T, dfeed).astype(BF16)
+        d_up[:, lo : lo + 768] = dot(hidden2_t, dupper).astype(BF16)
         db_up.append(total(dupper.astype(F32)))
-        dhidden2 = dhidden2 + dot(dupper, w_up[:, lo : lo + D], 1, 1)
+        dhidden2 = dhidden2 + dot(dupper, w_up[:, lo : lo + 768], 1, 1)
     feed = feed + b_lower
     result[0] = (middle + gate2 * feed).astype(BF16)
     dgate2 = total(g * feed)

time: 68.3 us -> 67.4 us (0.987)
  Pallas kernels: 66.5 us -> 65.6 us
    pallas_call x1, Pallas kernels: 64.5 us -> 63.6 us  [local(): pl.pallas_call(block_kernel, out_shape=outs + [shape(24, D, dtype=F32), s...]
where the time goes in v5:
time: 67.4 us; the launch traced here: 66.4 us
  Pallas kernels  65.6 us (97%)
  between operations  0.82 us (1%)
    pallas_call x1, Pallas kernels, local(): pl.pallas_call(block_kernel, out_shape=outs + [shape(24, D, dtype=F32), s...  63.6 us
    pallas_call x1, Pallas kernels, local(): pl.pallas_call(unpack_kernel, out_shape=outs + grads, in_specs=whole(6),...  1.97 us

profile of v5, /device:TPU:1, one launch (start us, length us, event | category | flops | bytes accessed | tf_op | source)
XLA Modules:
  0.0 66.4 jit_solution(11727898193943237688)
XLA Ops:
  0.6 63.6 %shard_map.228 = (bf16[1,256,384]{2,1,0:T(8,128)(2,1)}, f32[1,256,384]{2,1,0:T(8,128)}, f32[1,384]{1,0:T(1,128)}, f32[24,384]{1,0:T(8,128)}, f32[16,384]{1,0:T(8,128)}, /*index=5*/f32[16,768]{1,0:T(8,128)}) custom-call(bf16[1,256,384]{2,1,0:T(8,128)(2,1)} %tokens.1, bf16[1,384]{1,0:T(2,128)(2,1)} %condition.1, bf16[1,3,2304]{2,1,0:T(4,128)(2,1)} %mod.1, ...), custom_call_target="tpu_custom_call" | custom-call | tf_op jit(solution)/shard_map/pallas_call | solution.py:602
  64.3 2.0 %shard_map.229 = (bf16[1,256,384]{2,1,0:T(8,128)(2,1)}, f32[1,256,384]{2,1,0:T(8,128)}, f32[1,384]{1,0:T(1,128)}, f32[3,1,2304]{2,1,0:T(1,128)}, f32[1,18]{1,0:T...) custom-call(bf16[1,256,384]{2,1,0:T(8,128)(2,1)} %get-tuple-element., ...), custom_call_target="tpu_custom_call" | custom-call | tf_op jit(solution)/shard_map/pallas_call | solution.py:629
